TPU v7x, 32 devices: a whole 2x2x4 slice. The times are simulated.
32 devices in a mesh: dp: 4 (over z), seq: 8 (over y, x, core).
Axes of the slice: x: 2, y: 2, z: 4, core: 2. Of those that a mesh axis runs over, the one named last changes fastest.
Arguments:
- tokens: bfloat16 [8192, 2048], P(('dp', 'seq')), may hold values from -6 to 6
- weights: bfloat16 [2048, 24576], P('dp'), may hold values from -1 to 1
- ln_gain: float32 [2, 2048], replicated, may hold values from 0.5 to 1.5
- ln_bias: float32 [2, 2048], replicated, may hold values from -1 to 1
- doc_starts: int32 [4, 4], P('dp'), may hold values from 0 to 2047, as said below
- cotangent: bfloat16 [8192, 2048], P(('dp', 'seq')), may hold values from -6 to 6
Outputs:
- output: bfloat16 [8192, 2048], P(('dp', 'seq'))
- grad_tokens: float32 [8192, 2048], P(('dp', 'seq'))
- grad_weights: float32 [2048, 24576], P(('dp', 'seq'))
- grad_gain: float32 [2, 2048], replicated
- grad_bias: float32 [2, 2048], replicated
Inputs may be any that keep to these rules, and one draw needn't show every extreme that they name: `doc_starts`: the first entry of each row is 0; entries do not fall along a row and may repeat.
All inputs are finite; a program needn't handle non-finite values.
Results may differ from a plain program's by a relative error of at most 0.014.
The roundings to bfloat16 on the way count: a program that leaves them out, or rounds other values in their place, can miss the bound.
Values may be sent and summed in bfloat16 or wider, within the bound.
A program may use at most 832 MiB of HBM per device.

v0:
```python
import jax
import jax.numpy as jnp
from jax import lax
from jax.sharding import PartitionSpec as P

HEADS = 8
QK = 256
VD = 512
FF = 4096


norm_eps = 1e-05
highest = lax.Precision.HIGHEST


def prefix(x, axis, combine, identity, reverse):
    devices, place = (lax.axis_size(axis), lax.axis_index(axis))
    everything = jax.tree.map(lambda part: lax.all_gather(part, axis), x)
    start = jax.tree.map(
        lambda part, zero: jnp.broadcast_to(jnp.asarray(zero, part.dtype), part.shape), x, identity
    )

    def step(k, before):
        at = devices - 1 - k if reverse else k
        reached = at > place if reverse else at < place
        new = combine(before, jax.tree.map(lambda part: part[at], everything))
        return jax.tree.map(lambda a, b: jnp.where(reached, a, b), new, before)

    return lax.fori_loop(0, devices, step, start)


def layer_norm(values, gain, shift):
    centre = jnp.mean(values, axis=-1, keepdims=True)
    centred = values - centre
    spread = jnp.mean(centred * centred, axis=-1, keepdims=True)
    return centred * lax.rsqrt(spread + norm_eps) * gain + shift


def group_norm(values):
    centre = jnp.mean(values, axis=-1, keepdims=True)
    centred = values - centre
    spread = jnp.mean(centred * centred, axis=-1, keepdims=True)
    return centred * lax.rsqrt(spread + norm_eps)


def gelu_tanh(values):
    return jax.nn.gelu(values, approximate=True)


def gating(gate_values, normed):
    return jax.nn.silu(gate_values) * normed


def rotate(values, positions, heads_count):
    length = values.shape[0]
    shaped = values.reshape(length, heads_count, -1)
    half_size = shaped.shape[-1] // 2
    inverse = 10000.0 ** (-(jnp.arange(half_size, dtype=jnp.float32) / half_size))
    angles = positions.astype(jnp.float32)[:, None] * inverse[None, :]
    cosine = jnp.cos(angles)[:, None, :]
    sine = jnp.sin(angles)[:, None, :]
    front = shaped[..., :half_size]
    back_half = shaped[..., half_size:]
    turned = jnp.concatenate(
        [front * cosine - back_half * sine, back_half * cosine + front * sine], axis=-1
    )
    return turned.reshape(length, -1)


def decay_tables(segs, seg_prev, heads_count):
    length = segs.shape[0]
    logs = jnp.log1p(-(2.0 ** (-5.0 - jnp.arange(heads_count, dtype=jnp.float32))))
    local = jnp.arange(length, dtype=jnp.int32)
    gap = (local[:, None] - local[None, :]).astype(jnp.float32)
    same = (segs[:, None] == segs[None, :]) & (local[:, None] >= local[None, :])
    within = jnp.where(
        same[None], jnp.exp(jnp.where(same[None], gap[None] * logs[:, None, None], 0.0)), 0.0
    )
    reach = jnp.where(
        (segs == seg_prev)[None, :],
        jnp.exp((local + 1).astype(jnp.float32)[None, :] * logs[:, None]),
        0.0,
    )
    ending = jnp.where(
        (segs == segs[-1])[None, :],
        jnp.exp((length - 1 - local).astype(jnp.float32)[None, :] * logs[:, None]),
        0.0,
    )
    carry = jnp.where(segs[-1] == seg_prev, jnp.exp(length * logs), 0.0)
    return (within, reach.T, ending.T, carry)


def combine_states(earlier, later):
    return (later[0] + later[1][:, None, None] * earlier[0], earlier[1] * later[1])


def contract_last(left, right):
    return lax.dot_general(
        left, right, (((1,), (1,)), ((), ())), preferred_element_type=jnp.float32
    )


def per_device(tokens, weights, ln_gain, ln_bias, doc_starts, cotangent):
    full = lax.all_gather(weights, "dp", axis=0, tiled=True)
    query_width = HEADS * QK
    value_width = HEADS * VD
    mixer_cols = 2 * query_width + 2 * value_width
    ffn_end = mixer_cols + FF
    out_end = ffn_end + value_width
    block = tokens.shape[0]
    offset = lax.axis_index("seq") * block
    positions = offset + jnp.arange(block, dtype=jnp.int32)
    starts = doc_starts[0]
    segs = jnp.sum((starts[None, :] <= positions[:, None]).astype(jnp.int32), axis=1)
    seg_prev = jnp.sum((starts <= offset - 1).astype(jnp.int32))
    within, reach, ending, carry = decay_tables(segs, seg_prev, HEADS)
    inputs = tokens.astype(jnp.float32)
    first, first_pull = jax.vjp(layer_norm, inputs, ln_gain[0], ln_bias[0])
    first_low = first.astype(jnp.bfloat16)
    project = jnp.dot(first_low, full[:, :mixer_cols], preferred_element_type=jnp.float32)

    def rotate_here(values):
        return rotate(values, positions, HEADS)

    query_rot, rotate_pull = jax.vjp(rotate_here, project[:, :query_width])
    query_low = query_rot.astype(jnp.bfloat16).reshape(block, HEADS, QK)
    key_low = (
        rotate_here(project[:, query_width : 2 * query_width])
        .astype(jnp.bfloat16)
        .reshape(block, HEADS, QK)
    )
    value_low = (
        project[:, 2 * query_width : 2 * query_width + value_width]
        .astype(jnp.bfloat16)
        .reshape(block, HEADS, VD)
    )
    gate_raw = project[:, 2 * query_width + value_width : mixer_cols]
    scores = jnp.einsum("thd,shd->hts", query_low, key_low, preferred_element_type=jnp.float32)
    attn_low = (scores * within).astype(jnp.bfloat16)
    intra = jnp.einsum("hts,shv->thv", attn_low, value_low, preferred_element_type=jnp.float32)
    key_scaled = key_low.astype(jnp.float32) * ending[:, :, None]
    value_wide = value_low.astype(jnp.float32)
    own_state = jnp.einsum("thd,thv->hdv", key_scaled, value_wide, precision=highest)
    incoming = prefix(
        (own_state, carry),
        "seq",
        combine_states,
        (jnp.zeros_like(own_state), jnp.ones_like(carry)),
        False,
    )[0]
    state_low = incoming.astype(jnp.bfloat16)
    across = (
        jnp.einsum("thd,hdv->thv", query_low, state_low, preferred_element_type=jnp.float32)
        * reach[:, :, None]
    )
    mixed = intra + across
    grouped, group_pull = jax.vjp(group_norm, mixed)
    gated, gating_pull = jax.vjp(gating, gate_raw, grouped.reshape(block, value_width))
    gated_low = gated.astype(jnp.bfloat16)
    hidden = inputs + contract_last(gated_low, full[:, ffn_end:out_end])
    second, second_pull = jax.vjp(layer_norm, hidden, ln_gain[1], ln_bias[1])
    second_low = second.astype(jnp.bfloat16)
    inner = jnp.dot(second_low, full[:, mixer_cols:ffn_end], preferred_element_type=jnp.float32)
    active, active_pull = jax.vjp(gelu_tanh, inner)
    active_low = active.astype(jnp.bfloat16)
    result = (hidden + contract_last(active_low, full[:, out_end:])).astype(jnp.bfloat16)
    grad_active = jnp.dot(cotangent, full[:, out_end:], preferred_element_type=jnp.float32)
    grad_inner_low = active_pull(grad_active)[0].astype(jnp.bfloat16)
    grad_second = contract_last(grad_inner_low, full[:, mixer_cols:ffn_end])
    grad_hidden_ln, gain_two, bias_two = second_pull(grad_second)
    grad_hidden = cotangent.astype(jnp.float32) + grad_hidden_ln
    grad_branch_low = grad_hidden.astype(jnp.bfloat16)
    grad_gated = jnp.dot(
        grad_branch_low, full[:, ffn_end:out_end], preferred_element_type=jnp.float32
    )
    grad_gate, grad_grouped = gating_pull(grad_gated)
    grad_mixed_low = group_pull(grad_grouped.reshape(block, HEADS, VD))[0].astype(jnp.bfloat16)
    grad_attn = jnp.einsum(
        "thv,shv->hts", grad_mixed_low, value_low, preferred_element_type=jnp.float32
    )
    grad_scores_low = (grad_attn * within).astype(jnp.bfloat16)
    grad_query = jnp.einsum(
        "hts,shd->thd", grad_scores_low, key_low, preferred_element_type=jnp.float32
    )
    grad_query = (
        grad_query
        + jnp.einsum("thv,hdv->thd", grad_mixed_low, state_low, preferred_element_type=jnp.float32)
        * reach[:, :, None]
    )
    grad_key = jnp.einsum(
        "hts,thd->shd", grad_scores_low, query_low, preferred_element_type=jnp.float32
    )
    grad_value = jnp.einsum(
        "hts,thv->shv", attn_low, grad_mixed_low, preferred_element_type=jnp.float32
    )
    grad_state = jnp.einsum(
        "thd,thv->hdv",
        query_low.astype(jnp.float32) * reach[:, :, None],
        grad_mixed_low.astype(jnp.float32),
        precision=highest,
    )
    grad_own = prefix(
        (grad_state, carry),
        "seq",
        combine_states,
        (jnp.zeros_like(grad_state), jnp.ones_like(carry)),
        True,
    )[0]
    grad_key = (
        grad_key
        + jnp.einsum("thv,hdv->thd", value_wide, grad_own, precision=highest) * ending[:, :, None]
    )
    grad_value = grad_value + jnp.einsum("thd,hdv->thv", key_scaled, grad_own, precision=highest)
    grad_query_raw = rotate_pull(grad_query.reshape(block, query_width))[0]
    grad_key_raw = rotate_pull(grad_key.reshape(block, query_width))[0]
    grad_project_low = jnp.concatenate(
        [
            grad_query_raw.astype(jnp.bfloat16),
            grad_key_raw.astype(jnp.bfloat16),
            grad_value.reshape(block, value_width).astype(jnp.bfloat16),
            grad_gate.astype(jnp.bfloat16),
        ],
        axis=1,
    )
    grad_first = contract_last(grad_project_low, full[:, :mixer_cols])
    grad_input_ln, gain_one, bias_one = first_pull(grad_first)
    grad_tokens = grad_hidden + grad_input_ln
    contract = (((0,), (0,)), ((), ()))
    pieces = [
        lax.dot_general(first_low, grad_project_low, contract, preferred_element_type=jnp.float32),
        lax.dot_general(second_low, grad_inner_low, contract, preferred_element_type=jnp.float32),
        lax.dot_general(grad_branch_low, gated_low, contract, preferred_element_type=jnp.float32),
        lax.dot_general(cotangent, active_low, contract, preferred_element_type=jnp.float32),
    ]
    grad_weights = lax.psum_scatter(
        jnp.concatenate(pieces, axis=1), ("dp", "seq"), scatter_dimension=0, tiled=True
    )
    grad_gain, grad_bias = lax.psum(
        (jnp.stack([gain_one, gain_two]), jnp.stack([bias_one, bias_two])), ("dp", "seq")
    )
    return (result, grad_tokens, grad_weights, grad_gain, grad_bias)


def solution(mesh):
    placed = (
        P(("dp", "seq"), None),
        P("dp", None),
        P(),
        P(),
        P("dp", None),
        P(("dp", "seq"), None),
    )
    return jax.shard_map(
        per_device,
        mesh=mesh,
        in_specs=placed,
        out_specs=(
            P(("dp", "seq"), None),
            P(("dp", "seq"), None),
            P(("dp", "seq"), None),
            P(),
            P(),
        ),
        check_vma=False,
    )
```

profile of v0, /device:TPU:0, one launch (start us, length us, event | category | flops | bytes accessed | tf_op | source)
XLA Modules:
  0.0 4068.6 jit_solution(5302845203135893930)
XLA Ops:
  12.1 1660.1 %all-gather.7.cloned.1.call-done = bf16[2048,24576]{1,0:T(8,128)(2,1)} async-done(((bf16[512,24576]{1,0:T(8,128)(2,1)}), bf16[2048,24576]{1,0:T(8,128)(2,1)}) %all-gather.7.cloned.1.call-update) | async-done | bytes 100663312 | tf_op jit(solution)/shard_map/all_gather | solution.py:104
  1672.2 26.0 fusion.4
  1698.2 2.5 slice.117
  1700.6 2.5 fusion.101
  1705.2 1.8 subtract_convert_fusion.1
  1708.0 4.4 fusion.57
  1713.8 8.7 all-gather.2
  1722.6 2.5 multiply_convert_fusion.3
  1726.1 2.8 fusion.51
  1728.9 142.6 %all-gather.9.cloned.1.call-done = f32[64,256,512]{2,1,0:T(8,128)} async-done(((f32[8,256,512]{2,1,0:T(8,128)}), f32[64,256,512]{2,1,0:T(8,128)}) %all-gather.9.cloned.1.call-update) | async-done | bytes 33554448 | tf_op jit(solution)/shard_map/all_gather | solution.py:18
  1871.5 51.6 %while.30 = (s32[]{:T(128)}, f32[8,256,512]{2,1,0:T(8,128)}, s32[]{:T(128)}, f32[8,8,256,512]{3,2,1,0:T(8,128)}, f32[8,8]{1,0:T(8,128)S(1)}, /*index=5*/s32[]{:T(128)}, s32[]{:T(128)}) while((s32[]{:T(128)}, f32[8,256,512]{2,1,0:T(8,128)}, s32[]{:T(128)}, f32[8,8,256,512]{3,2,1,0:T(8,128)}, f32[8,8]{1,0:T(8,128)S(1)}, ...), condition=%wide.region_5.6_spmd.clone, body=%wide.region_4.5_spmd.clone.sunk | while | flops 4194308 | bytes 12583121 | solution.py:29
  1871.7 5.3 fusion.129
  1877.0 6.6 fusion.129
  1883.6 6.6 fusion.129
  1890.2 6.6 fusion.129
  1896.8 6.6 fusion.129
  1903.4 6.6 fusion.129
  1910.0 6.6 fusion.129
  1916.6 6.6 fusion.129
  1923.2 4.8 fusion.106
  1930.0 2.5 subtract_multiply_fusion.1
  1932.5 5.7 copy.109
  1938.2 6.0 multiply_convert_fusion.1
  1944.2 12.3 fusion.107
  1956.5 2.1 multiply_reduce_fusion.4
  1958.7 8.3 fusion.12
  1967.0 11.5 fusion.24
  1978.6 10.0 multiply_reduce_fusion.2
  1990.6 1.6 copy-done.16
  1992.2 12.0 fusion.84
  2004.2 6.0 copy.111
  2010.2 4.2 multiply_reduce_fusion
  2019.4 5.9 fusion.61
  2025.4 2.9 multiply_convert_fusion.2
  2028.3 1.9 fusion.94
  2032.7 1.8 fusion.60
  2035.9 14.4 fusion.108
  2050.3 13.3 convolution_bitcast_fusion
  2063.6 13.3 fusion.98
  2077.0 109.3 %all-gather.11.cloned.1.call-done = f32[64,256,512]{2,1,0:T(8,128)} async-done(((f32[8,256,512]{2,1,0:T(8,128)}), f32[64,256,512]{2,1,0:T(8,128)}) %all-gather.11.cloned.1.call-update) | async-done | bytes 33554448 | tf_op jit(solution)/shard_map/all_gather | solution.py:18
  2186.3 56.7 %while.31 = (s32[]{:T(128)}, f32[8,256,512]{2,1,0:T(8,128)}, s32[]{:T(128)}, f32[8,8,256,512]{3,2,1,0:T(8,128)}, f32[8,8]{1,0:T(8,128)}, /*index=5*/s32[]{:T(128)}, s32[]{:T(128)}, s32[]{:T(128)}, s32[]{:T(128)}) while((s32[]{:T(128)}, f32[8,256,512]{2,1,0:T(8,128)}, s32[]{:T(128)}, f32[8,8,256,512]{3,2,1,0:T(8,128)}, ...), condition=%wide.region_15.16_spmd.clone, body=%wide.region_14.15_spmd.clone.sunk | while | flops 4194312 | bytes 12583183 | solution.py:29
  2187.0 5.3 fusion.130
  2193.0 6.5 fusion.130
  2200.2 6.5 fusion.130
  2207.5 6.5 fusion.130
  2214.7 6.5 fusion.130
  2221.9 6.5 fusion.130
  2229.2 6.5 fusion.130
  2236.4 6.5 fusion.130
  2243.0 9.3 fusion.64
  2252.3 2.4 fusion.59
  2254.8 2.0 add_convert_fusion
  2256.9 1.9 multiply_add_fusion.3
  2260.0 2.9 copy.110
  2263.0 2.4 fusion.76
  2266.6 37.1 fusion.74
  2303.6 159.9 %pad_maximum_fusion = f32[2048,24576]{1,0:T(8,128)} fusion(f32[2048,4096]{1,0:T(8,128)} %convolution_bitcast_fusion, f32[2048,4096]{1,0:T(8,128)} %fusion.108, f32[2048,4096]{1,0:T(8,128)} %fusion.98, f32[2048,12288]{1,0:T(8,128)} %fusion.74), kind=kLoop, calls=%fused_computation.6 | loop fusion | flops 150994944 | bytes 402653184 | tf_op jit(solution)/shard_map/concatenate | solution.py:236
  2463.5 1.6 copy-done.13
  2465.1 15.2 fusion.41
  2480.4 34.6 fusion.99
  2515.1 3.1 fusion.48
  2518.2 39.9 all-reduce.4
  2558.1 4.8 add_add_fusion.3
  2563.0 1498.7 %reduce-scatter.2.cloned.1.call-done = f32[64,24576]{1,0:T(8,128)} async-done(((f32[2048,24576]{1,0:T(8,128)}), f32[64,24576]{1,0:T(8,128)}) %reduce-scatter.2.cloned.1.call-update) | async-done | bytes 6291472 | tf_op jit(solution)/shard_map/reduce_scatter | solution.py:235
  (201 shorter events, 30.0 us)
Async XLA Ops:
  7.2 2.2 copy-start.8
  7.2 1665.0 %all-gather.7.cloned.1.call-start = ((), (), s32[]{:S(2)}) async-start(), calls=%async_computation.1 | async-start | bytes 125829120 | tf_op jit(solution)/shard_map/all_gather | solution.py:104
  7.9 4.1 copy-start.57
  7.9 4.1 copy-start.58
  7.9 1863.6 %all-gather.9.cloned.1.call-start = ((), (), s32[]{:S(2)}) async-start(), calls=%async_computation.3 | async-start | bytes 37748736 | tf_op jit(solution)/shard_map/all_gather | solution.py:18
  9.6 1662.6 %copy-start.49 = (f32[256]{0:T(256)}, f32[256]{0:T(256)S(1)}, u32[]{:S(2)}) copy-start(f32[256]{0:T(256)S(1)} %broadcast_multiply_fusion.2) | copy-start | bytes 3076
  10.0 1.4 copy-start.61
  10.0 1662.2 %copy-start.52 = (f32[256]{0:T(256)}, f32[256]{0:T(256)S(1)}, u32[]{:S(2)}) copy-start(f32[256]{0:T(256)S(1)} %fusion.87) | copy-start | bytes 3076
  11.4 1695.6 %copy-start.55 = (f32[256,8]{0,1:T(8,128)}, f32[256,8]{0,1:T(8,128)S(1)}, u32[]{:S(2)}) copy-start(f32[256,8]{0,1:T(8,128)S(1)} %get-tuple-element.328) | copy-start | bytes 24580
  12.0 1693.2 %copy-start.40 = (f32[256,128]{1,0:T(8,128)}, f32[256,128]{1,0:T(8,128)S(1)}, u32[]{:S(2)}) copy-start(f32[256,128]{1,0:T(8,128)S(1)} %get-tuple-element.324) | copy-start | bytes 393220
  12.0 1693.2 %copy-start.42 = (f32[256,128]{1,0:T(8,128)}, f32[256,128]{1,0:T(8,128)S(1)}, u32[]{:S(2)}) copy-start(f32[256,128]{1,0:T(8,128)S(1)} %get-tuple-element.325) | copy-start | bytes 393220
  12.1 1660.2 %copy-start.44 = (f32[1,2048]{1,0:T(1,128)}, f32[1,2048]{1,0:T(1,128)S(1)}, u32[]{:S(2)}) copy-start(f32[1,2048]{1,0:T(1,128)S(1)} %get-tuple-element.321) | copy-start | bytes 24580
  12.1 1660.1 %copy-start.47 = (f32[1,2048]{1,0:T(1,128)}, f32[1,2048]{1,0:T(1,128)S(1)}, u32[]{:S(2)}) copy-start(f32[1,2048]{1,0:T(1,128)S(1)} %get-tuple-element.323) | copy-start | bytes 24580
  1712.4 473.9 %all-gather.11.cloned.1.call-start = ((), (), s32[]{:S(2)}) async-start(), calls=%async_computation.4 | async-start | bytes 37748736 | tf_op jit(solution)/shard_map/all_gather | solution.py:18
  1923.2 4.8 copy-start.65
  1928.0 2.0 copy-start.2
  1956.5 2.2 copy-start.11
  1958.7 8.3 copy-start.17
  1967.0 11.6 copy-start.32
  1978.6 10.0 copy-start.38
  1989.3 1.3 copy-start.14
  1989.3 2.9 copy-start.16
  1992.2 12.0 copy-start.34
  2010.2 4.6 copy-start.3
  2010.2 5.9 copy-start.4
  2017.0 2.4 copy-start.28
  2017.0 2.4 copy-start.30
  2025.3 2036.3 %reduce-scatter.2.cloned.1.call-start = ((), (), s32[]{:S(2)}) async-start(), calls=%async_computation.2 | async-start | bytes 207618048 | tf_op jit(solution)/shard_map/reduce_scatter | solution.py:235
  2025.4 2.9 copy-start.29
  2025.4 2.9 copy-start.31
  2025.4 4.8 copy-start.6
  2028.3 2.9 copy-start
  2031.3 1.4 copy-start.26
  2032.7 2.8 copy-start.18
  2032.7 3.3 copy-start.35
  2035.9 14.4 copy-start.33
  2050.3 13.3 copy-start.12
  2050.3 13.3 copy-start.39
  2186.3 56.7 %copy-start.24 = (bf16[256,8,128]{2,0,1:T(8,128)(2,1)S(1)}, bf16[256,8,128]{2,0,1:T(8,128)(2,1)}, u32[]{:S(2)}) copy-start(bf16[256,8,128]{2,0,1:T(8,128)(2,1)} %copy-done.22) | copy-start | bytes 1572868
  2186.3 56.7 %copy-start.27 = (bf16[256,8,128]{2,0,1:T(8,128)(2,1)S(1)}, bf16[256,8,128]{2,0,1:T(8,128)(2,1)}, u32[]{:S(2)}) copy-start(bf16[256,8,128]{2,0,1:T(8,128)(2,1)} %copy-done.25) | copy-start | bytes 1572868
  2186.3 56.7 %copy-start.56 = (f32[256,8]{0,1:T(8,128)S(1)}, f32[256,8]{0,1:T(8,128)}, u32[]{:S(2)}) copy-start(f32[256,8]{0,1:T(8,128)} %copy-done.55) | copy-start | bytes 24580
  2242.9 9.4 copy-start.1
  2242.9 9.4 copy-start.21
  2252.3 2.4 copy-start.7
  2252.3 2.4 copy-start.37
  2254.8 2.1 copy-start.20
  2254.8 2.1 copy-start.41
  2254.8 2.0 copy-start.43
  2262.9 3.6 copy-start.19
  2263.0 3.6 copy-start.9
  2263.0 3.6 copy-start.45
  2263.0 3.6 copy-start.48
  2263.0 3.6 copy-start.50
  2263.0 3.6 copy-start.53
  2463.5 1.6 copy-start.13
  2465.1 15.2 copy-start.10
  2465.1 15.2 copy-start.46
  2465.1 15.2 copy-start.51
  2480.3 34.6 copy-start.62
  2480.4 34.7 copy-start.64
  2480.4 34.7 copy-start.54
  2515.0 3.2 copy-start.63
  2515.0 43.1 %copy-start.15 = (f32[256,2048]{1,0:T(8,128)S(1)}, f32[256,2048]{1,0:T(8,128)}, u32[]{:S(2)}) copy-start(f32[256,2048]{1,0:T(8,128)} %copy-done.14) | copy-start | bytes 6291460
  2515.0 43.1 %copy-start.60 = (f32[256]{0:T(256)S(1)}, f32[256]{0:T(256)}, u32[]{:S(2)}) copy-start(f32[256]{0:T(256)} %copy-done.59) | copy-start | bytes 3076
  (7 other events, 7.4 us)
Sparse Core Ops, SparseCore 0:
  9.6 1662.5 all-gather.6
  1712.5 158.9 all-gather.8
  2025.4 160.7 all-gather.10
  2463.7 1597.9 reduce-scatter.1
where the time goes:
time: 4080 us; the launch traced here: 4070 us
  waiting for transfers between devices  3410 us (84%)
  other arithmetic  298 us (7%)
  matrix products  249 us (6%)
  blocking collectives  48.6 us (1%)
  local copies, waits for them, and re-layouts  44.1 us (1%)
    all_gather x1, waiting for transfers between devices, per_device(): full = lax.all_gather(weights, 'dp', axis=0, tiled=True)  1660 us
    reduce_scatter x1, waiting for transfers between devices, per_device(): lax.psum_scatter(jnp.concatenate(pieces, axis=1), ('dp', 'seq'), scatter_...  1500 us
    all_gather x2, waiting for transfers between devices, prefix(): everything = jax.tree.map(lambda part: lax.all_gather(part, axis), x)  252 us
    concatenate x1, other arithmetic, per_device(): jnp.concatenate(pieces, axis=1)  160 us
    select_n x16, other arithmetic, step(): return jax.tree.map(lambda a, b: jnp.where(reached, a, b), new, before)  102 us
  transfers between devices with their start and end apart: 4, of which 4 were waited for; matrix products, arithmetic and copies ran while one was open for 3% of the time, Pallas kernels for 0%

commit v1 on v0

--- a/solution.py
+++ b/solution.py
@@ -11,6 +11,8 @@
 
 norm_eps = 1e-05
 highest = lax.Precision.HIGHEST
+f32 = jnp.float32
+bf16 = jnp.bfloat16
 
 
 def prefix(x, axis, combine, identity, reverse):
@@ -67,9 +69,12 @@
     return turned.reshape(length, -1)
 
 
-def decay_tables(segs, seg_prev, heads_count):
+def head_logs():
+    return jnp.log1p(-(2.0 ** (-5.0 - jnp.arange(HEADS, dtype=jnp.float32))))
+
+
+def decay_tables(segs, seg_prev, logs):
     length = segs.shape[0]
-    logs = jnp.log1p(-(2.0 ** (-5.0 - jnp.arange(heads_count, dtype=jnp.float32))))
     local = jnp.arange(length, dtype=jnp.int32)
     gap = (local[:, None] - local[None, :]).astype(jnp.float32)
     same = (segs[:, None] == segs[None, :]) & (local[:, None] >= local[None, :])
@@ -100,7 +105,7 @@
     )
 
 
-def per_device(tokens, weights, ln_gain, ln_bias, doc_starts, cotangent):
+def per_device_spread(tokens, weights, ln_gain, ln_bias, doc_starts, cotangent):
     full = lax.all_gather(weights, "dp", axis=0, tiled=True)
     query_width = HEADS * QK
     value_width = HEADS * VD
@@ -113,7 +118,7 @@
     starts = doc_starts[0]
     segs = jnp.sum((starts[None, :] <= positions[:, None]).astype(jnp.int32), axis=1)
     seg_prev = jnp.sum((starts <= offset - 1).astype(jnp.int32))
-    within, reach, ending, carry = decay_tables(segs, seg_prev, HEADS)
+    within, reach, ending, carry = decay_tables(segs, seg_prev, head_logs())
     inputs = tokens.astype(jnp.float32)
     first, first_pull = jax.vjp(layer_norm, inputs, ln_gain[0], ln_bias[0])
     first_low = first.astype(jnp.bfloat16)
@@ -241,6 +246,195 @@
     return (result, grad_tokens, grad_weights, grad_gain, grad_bias)
 
 
+def sections(n_seq):
+    widths = (HEADS * QK, HEADS * QK, HEADS * VD, HEADS * VD, FF, HEADS * VD, FF)
+    start, out = 0, []
+    for width in widths:
+        out.append((start, width // n_seq))
+        start += width
+    return out
+
+
+def per_device_heads(tokens, weights, ln_gain, ln_bias, doc_starts, cotangent):
+    n_seq, place = lax.axis_size("seq"), lax.axis_index("seq")
+    heads = HEADS // n_seq
+    block = tokens.shape[0]
+    length = block * n_seq
+    secs = sections(n_seq)
+
+    def gather_weights(which):
+        part = jnp.concatenate(
+            [
+                lax.dynamic_slice_in_dim(weights, start + place * width, width, axis=1)
+                for start, width in (secs[i] for i in which)
+            ],
+            axis=1,
+        )
+        return lax.all_gather(part, "dp", axis=0, tiled=True)
+
+    w_qk = gather_weights((0, 1))
+    w_v = gather_weights((2,))
+    w_g = gather_weights((3,))
+    w_out = gather_weights((5,))
+    w_in = gather_weights((4,))
+    w_down = gather_weights((6,))
+
+    def row_gather(part):
+        return lax.all_gather(part, "seq", axis=0, tiled=True)
+
+    def row_scatter(full):
+        return lax.psum_scatter(
+            full.astype(bf16), "seq", scatter_dimension=0, tiled=True
+        ).astype(f32)
+
+    positions = jnp.arange(length, dtype=jnp.int32)
+    starts = doc_starts[0]
+    segs = jnp.sum((starts[None, :] <= positions[:, None]).astype(jnp.int32), axis=1)
+    seg_blocks = segs.reshape(n_seq, block)
+    seg_before = jnp.concatenate([jnp.zeros((1,), jnp.int32), seg_blocks[:-1, -1]])
+    inputs = tokens.astype(f32)
+    first, first_pull = jax.vjp(layer_norm, inputs, ln_gain[0], ln_bias[0])
+    first_low = row_gather(first.astype(bf16))
+    cot_low = row_gather(cotangent)
+    qk_raw = jnp.dot(first_low, w_qk, preferred_element_type=f32)
+
+    def rotate_here(values):
+        return rotate(values, positions, heads)
+
+    query_rot, rotate_pull = jax.vjp(rotate_here, qk_raw[:, : heads * QK])
+
+    def blocked(values):
+        return values.reshape(n_seq, block, heads, -1)
+
+    query_low = blocked(query_rot.astype(bf16))
+    key_low = blocked(rotate_here(qk_raw[:, heads * QK :]).astype(bf16))
+    value_low = blocked(jnp.dot(first_low, w_v, preferred_element_type=f32).astype(bf16))
+    gate_raw = jnp.dot(first_low, w_g, preferred_element_type=f32)
+    logs = lax.dynamic_slice_in_dim(head_logs(), place * heads, heads)
+    within, reach, ending, carry = jax.vmap(decay_tables, (0, 0, None))(
+        seg_blocks, seg_before, logs
+    )
+    scores = jnp.einsum("bthd,bshd->bhts", query_low, key_low, preferred_element_type=f32)
+    attn_low = (scores * within).astype(bf16)
+    intra = jnp.einsum("bhts,bshv->bthv", attn_low, value_low, preferred_element_type=f32)
+    key_scaled = key_low.astype(f32) * ending[..., None]
+    value_wide = value_low.astype(f32)
+    own_state = jnp.einsum("bthd,bthv->bhdv", key_scaled, value_wide, precision=highest)
+    state = jnp.zeros_like(own_state[0])
+    states = []
+    for b in range(n_seq):
+        states.append(state.astype(bf16))
+        state = own_state[b] + carry[b][:, None, None] * state
+    state_low = jnp.stack(states)
+    across = (
+        jnp.einsum("bthd,bhdv->bthv", query_low, state_low, preferred_element_type=f32)
+        * reach[..., None]
+    )
+    mixed = (intra + across).reshape(length, heads, VD)
+    grouped, group_pull = jax.vjp(group_norm, mixed)
+    gated, gating_pull = jax.vjp(gating, gate_raw, grouped.reshape(length, heads * VD))
+    gated_low = gated.astype(bf16)
+    hidden = inputs + row_scatter(contract_last(gated_low, w_out))
+    second, second_pull = jax.vjp(layer_norm, hidden, ln_gain[1], ln_bias[1])
+    second_low = row_gather(second.astype(bf16))
+    inner = jnp.dot(second_low, w_in, preferred_element_type=f32)
+    active, active_pull = jax.vjp(gelu_tanh, inner)
+    active_low = active.astype(bf16)
+    result = (hidden + row_scatter(contract_last(active_low, w_down))).astype(bf16)
+    contract = (((0,), (0,)), ((), ()))
+
+    def weight_grad(left, right):
+        return lax.psum_scatter(
+            lax.dot_general(left, right, contract, preferred_element_type=f32).astype(bf16),
+            "dp",
+            scatter_dimension=0,
+            tiled=True,
+        )
+
+    def spread(grad):
+        return lax.all_to_all(grad, "seq", 0, 1, tiled=True).astype(f32)
+
+    g_down = weight_grad(cot_low, active_low)
+    grad_active = jnp.dot(cot_low, w_down, preferred_element_type=f32)
+    grad_inner_low = active_pull(grad_active)[0].astype(bf16)
+    grad_second = row_scatter(contract_last(grad_inner_low, w_in))
+    g_in = weight_grad(second_low, grad_inner_low)
+    grad_hidden_ln, gain_two, bias_two = second_pull(grad_second)
+    grad_hidden = cotangent.astype(f32) + grad_hidden_ln
+    grad_branch_low = row_gather(grad_hidden.astype(bf16))
+    g_out = weight_grad(grad_branch_low, gated_low)
+    grad_gated = jnp.dot(grad_branch_low, w_out, preferred_element_type=f32)
+    grad_gate, grad_grouped = gating_pull(grad_gated)
+    grad_gate_low = grad_gate.astype(bf16)
+    g_g = weight_grad(first_low, grad_gate_low)
+    grad_mixed_low = blocked(group_pull(grad_grouped.reshape(length, heads, VD))[0].astype(bf16))
+    grad_attn = jnp.einsum(
+        "bthv,bshv->bhts", grad_mixed_low, value_low, preferred_element_type=f32
+    )
+    grad_scores_low = (grad_attn * within).astype(bf16)
+    grad_query = jnp.einsum(
+        "bhts,bshd->bthd", grad_scores_low, key_low, preferred_element_type=f32
+    )
+    grad_query = (
+        grad_query
+        + jnp.einsum("bthv,bhdv->bthd", grad_mixed_low, state_low, preferred_element_type=f32)
+        * reach[..., None]
+    )
+    grad_key = jnp.einsum(
+        "bhts,bthd->bshd", grad_scores_low, query_low, preferred_element_type=f32
+    )
+    grad_value = jnp.einsum(
+        "bhts,bthv->bshv", attn_low, grad_mixed_low, preferred_element_type=f32
+    )
+    grad_state = jnp.einsum(
+        "bthd,bthv->bhdv",
+        query_low.astype(f32) * reach[..., None],
+        grad_mixed_low.astype(f32),
+        precision=highest,
+    )
+    leave = jnp.zeros_like(grad_state[0])
+    leaves = [None] * n_seq
+    for b in reversed(range(n_seq)):
+        leaves[b] = leave
+        leave = grad_state[b] + carry[b][:, None, None] * leave
+    grad_own = jnp.stack(leaves)
+    grad_key = (
+        grad_key
+        + jnp.einsum("bthv,bhdv->bthd", value_wide, grad_own, precision=highest)
+        * ending[..., None]
+    )
+    grad_value = grad_value + jnp.einsum("bthd,bhdv->bthv", key_scaled, grad_own, precision=highest)
+    grad_v_low = grad_value.reshape(length, heads * VD).astype(bf16)
+    g_v = weight_grad(first_low, grad_v_low)
+    grad_query_raw = rotate_pull(grad_query.reshape(length, heads * QK))[0]
+    grad_key_raw = rotate_pull(grad_key.reshape(length, heads * QK))[0]
+    grad_qk_low = jnp.concatenate([grad_query_raw.astype(bf16), grad_key_raw.astype(bf16)], axis=1)
+    grad_first = row_scatter(
+        contract_last(grad_qk_low, w_qk)
+        + contract_last(grad_v_low, w_v)
+        + contract_last(grad_gate_low, w_g)
+    )
+    g_qk = weight_grad(first_low, grad_qk_low)
+    grad_input_ln, gain_one, bias_one = first_pull(grad_first)
+    grad_tokens = grad_hidden + grad_input_ln
+    grad_weights = jnp.concatenate(
+        [
+            spread(g_qk[:, : heads * QK]),
+            spread(g_qk[:, heads * QK :]),
+            spread(g_v),
+            spread(g_g),
+            spread(g_in),
+            spread(g_out),
+            spread(g_down),
+        ],
+        axis=1,
+    )
+    grad_gain, grad_bias = lax.psum(
+        (jnp.stack([gain_one, gain_two]), jnp.stack([bias_one, bias_two])), ("dp", "seq")
+    )
+    return (result, grad_tokens, grad_weights, grad_gain, grad_bias)
+
+
 def solution(mesh):
     placed = (
         P(("dp", "seq"), None),
@@ -250,8 +444,9 @@
         P("dp", None),
         P(("dp", "seq"), None),
     )
+    divides = HEADS % mesh.shape["seq"] == 0
     return jax.shard_map(
-        per_device,
+        per_device_heads if divides else per_device_spread,
         mesh=mesh,
         in_specs=placed,
         out_specs=(

time: 4080 us -> 1180 us (0.29)
  waiting for transfers between devices: 3410 us -> 760 us
  other arithmetic: 298 us -> 59.2 us
    all_gather x3 -> x10, waiting for transfers between devices: 1910 us -> 404 us  [the longest x6 206 us: gather_weights(): return lax.all_gather(part, 'dp', axis=0, tiled=True)]
    reduce_scatter x1 -> x10, waiting for transfers between devices: 1500 us -> 320 us  [the longest x4 251 us: row_scatter(): lax.psum_scatter(full.astype(bf16), 'seq', scatter_dimension=0, tiled=True)]
    concatenate x1 -> x4, other arithmetic: 160 us -> 7.33 us  [the longest x1 5.26 us: per_device_heads(): jnp.concatenate([spread(g_qk[:, :heads * QK]), spread(g_qk[:, heads * QK:...]
    select_n x17 -> x2, other arithmetic: 103 us -> 0.15 us  [the longest x1 0.07 us: decay_tables(): jnp.where((segs == seg_prev)[None, :], jnp.exp((local + 1).astype(jnp.flo...]
    dot_general x20 -> x24, matrix products: 177 us -> 147 us  [the longest x6 59.9 us: weight_grad(): lax.dot_general(left, right, contract, preferred_element_type=f32)]
  transfers between devices with their start and end apart: 4 -> 26, of which waited for: 4 -> 20; matrix products, arithmetic and copies ran while one was open for 3% -> 22% of each run, Pallas kernels for 0% -> 0%
where the time goes in v1:
time: 1180 us; the launch traced here: 1170 us
  waiting for transfers between devices  760 us (64%)
  matrix products  211 us (18%)
  other arithmetic  59.2 us (5%)
  blocking collectives  49.5 us (4%)
  local copies, waits for them, and re-layouts  49.3 us (4%)
  starting transfers between devices  23.2 us (2%)
  between operations  17.9 us (2%)
    reduce_scatter x4, waiting for transfers between devices, row_scatter(): lax.psum_scatter(full.astype(bf16), 'seq', scatter_dimension=0, tiled=True)  251 us
    all_gather x6, waiting for transfers between devices, gather_weights(): return lax.all_gather(part, 'dp', axis=0, tiled=True)  206 us
    all_gather x4, waiting for transfers between devices, row_gather(): return lax.all_gather(part, 'seq', axis=0, tiled=True)  199 us
    reduce_scatter x6, waiting for transfers between devices, weight_grad(): lax.psum_scatter(lax.dot_general(left, right, contract, preferred_element...  68.2 us
    dot_general x6, matrix products, contract_last(): lax.dot_general(left, right, (((1,), (1,)), ((), ())), preferred_element_...  63.6 us
    dot_general x6, matrix products, weight_grad(): lax.dot_general(left, right, contract, preferred_element_type=f32)  59.9 us
    psum x1, blocking collectives, per_device_heads(): lax.psum((jnp.stack([gain_one, gain_two]), jnp.stack([bias_one, bias_two]...  40.1 us
    all_to_all x6, waiting for transfers between devices, spread(): return lax.all_to_all(grad, 'seq', 0, 1, tiled=True).astype(f32)  32.5 us
  transfers between devices with their start and end apart: 26, of which 20 were waited for; matrix products, arithmetic and copies ran while one was open for 22% of the time, Pallas kernels for 0%

profile of v1, /device:TPU:0, one launch (start us, length us, event | category | flops | bytes accessed | tf_op | source)
XLA Modules:
  0.0 1169.6 jit_solution(8871564800417961883)
XLA Ops:
  12.2 3.2 constant_dynamic-slice_fusion.1
  22.1 36.2 %all-gather.17.cloned.1.call-done = bf16[2048,512]{1,0:T(8,128)(2,1)} async-done(((bf16[512,512]{1,0:T(8,128)(2,1)}), bf16[2048,512]{1,0:T(8,128)(2,1)}) %all-gather.17.cloned.1.call-update) | async-done | bytes 2097168 | tf_op jit(solution)/shard_map/all_gather | solution.py:273
  58.2 55.9 %all-gather.11.cloned.1.call-done = bf16[2048,2048]{1,0:T(8,128)(2,1)} async-done(((bf16[256,2048]{1,0:T(8,128)(2,1)}), bf16[2048,2048]{1,0:T(8,128)(2,1)}) %all-gather.11.cloned.1.call-update) | async-done | bytes 8388624 | tf_op jit(solution)/shard_map/all_gather | solution.py:283
  114.1 7.6 fusion.115
  122.1 4.8 fusion.72
  130.2 32.0 %all-gather.15.cloned.1.call-done = bf16[2048,512]{1,0:T(8,128)(2,1)} async-done(((bf16[512,512]{1,0:T(8,128)(2,1)}), bf16[2048,512]{1,0:T(8,128)(2,1)}) %all-gather.15.cloned.1.call-update) | async-done | bytes 2097168 | tf_op jit(solution)/shard_map/all_gather | solution.py:273
  162.3 8.5 convolution_convert_fusion.9
  170.8 2.6 fusion.45
  186.1 22.1 %all-gather.13.cloned.1.call-done = bf16[2048,512]{1,0:T(8,128)(2,1)} async-done(((bf16[512,512]{1,0:T(8,128)(2,1)}), bf16[2048,512]{1,0:T(8,128)(2,1)}) %all-gather.13.cloned.1.call-update) | async-done | bytes 2097168 | tf_op jit(solution)/shard_map/all_gather | solution.py:273
  208.2 10.1 multiply_convert_fusion.1
  218.3 36.0 %all-gather.19.cloned.1.call-done = bf16[2048,512]{1,0:T(8,128)(2,1)} async-done(((bf16[512,512]{1,0:T(8,128)(2,1)}), bf16[2048,512]{1,0:T(8,128)(2,1)}) %all-gather.19.cloned.1.call-update) | async-done | bytes 2097168 | tf_op jit(solution)/shard_map/all_gather | solution.py:273
  254.4 8.3 convolution_convert_fusion.2
  263.5 69.3 %reduce-scatter.11.cloned.1.call-done = bf16[256,2048]{1,0:T(8,128)(2,1)} async-done(((bf16[2048,2048]{1,0:T(8,128)(2,1)}), bf16[256,2048]{1,0:T(8,128)(2,1)}) %reduce-scatter.11.cloned.1.call-update) | async-done | bytes 1048592 | tf_op jit(solution)/shard_map/reduce_scatter | solution.py:286
  338.3 42.1 %all-gather.23.cloned.1.call-done = bf16[2048,512]{1,0:T(8,128)(2,1)} async-done(((bf16[512,512]{1,0:T(8,128)(2,1)}), bf16[2048,512]{1,0:T(8,128)(2,1)}) %all-gather.23.cloned.1.call-update) | async-done | bytes 2097168 | tf_op jit(solution)/shard_map/all_gather | solution.py:273
  380.4 55.8 %all-gather.21.cloned.1.call-done = bf16[2048,2048]{1,0:T(8,128)(2,1)} async-done(((bf16[256,2048]{1,0:T(8,128)(2,1)}), bf16[2048,2048]{1,0:T(8,128)(2,1)}) %all-gather.21.cloned.1.call-update) | async-done | bytes 8388624 | tf_op jit(solution)/shard_map/all_gather | solution.py:283
  436.2 10.5 fusion.116
  446.6 37.2 %all-gather.25.cloned.1.call-done = bf16[2048,512]{1,0:T(8,128)(2,1)} async-done(((bf16[512,512]{1,0:T(8,128)(2,1)}), bf16[2048,512]{1,0:T(8,128)(2,1)}) %all-gather.25.cloned.1.call-update) | async-done | bytes 2097168 | tf_op jit(solution)/shard_map/all_gather | solution.py:273
  483.8 55.0 %all-gather.27.cloned.1.call-done = bf16[2048,2048]{1,0:T(8,128)(2,1)} async-done(((bf16[256,2048]{1,0:T(8,128)(2,1)}), bf16[2048,2048]{1,0:T(8,128)(2,1)}) %all-gather.27.cloned.1.call-update) | async-done | bytes 8388624 | tf_op jit(solution)/shard_map/all_gather | solution.py:283
  538.8 12.3 %fusion.6 = bf16[2048,512]{1,0:T(8,128)(2,1)S(1)} fusion(f32[2048,512]{1,0:T(8,128)} %fusion.116, bf16[2048,2048]{1,0:T(8,128)(2,1)} %all-gather.27.cloned.1.call-done, bf16[2048,512]{1,0:T(8,128)(2,1)} %all-gather.25.cloned.1.call-done), kind=kOutput, calls=%fused_computation.14 | convolution fusion | flops 4315938816 | bytes 16777216 | tf_op jit(solution)/shard_map/dot_general | solution.py:358
  552.5 7.1 convolution_convert_fusion
  559.6 12.4 %convolution_convert_fusion.1 = bf16[2048,2048]{1,0:T(8,128)(2,1)} fusion(bf16[2048,512]{1,0:T(8,128)(2,1)} %all-gather.25.cloned.1.call-done, f32[2048,512]{1,0:T(8,128)} %fusion.116), kind=kOutput, calls=%fused_computation.2 | convolution fusion | flops 4308598784 | bytes 14680064 | tf_op jit(solution)/shard_map/dot_general | solution.py:103
  572.1 58.9 %reduce-scatter.15.cloned.1.call-done = bf16[256,2048]{1,0:T(8,128)(2,1)} async-done(((bf16[2048,2048]{1,0:T(8,128)(2,1)}), bf16[256,2048]{1,0:T(8,128)(2,1)}) %reduce-scatter.15.cloned.1.call-update) | async-done | bytes 1048592 | tf_op jit(solution)/shard_map/reduce_scatter | solution.py:286
  631.1 2.8 fusion.35
  633.8 71.9 %reduce-scatter.13.cloned.1.call-done = bf16[256,2048]{1,0:T(8,128)(2,1)} async-done(((bf16[2048,2048]{1,0:T(8,128)(2,1)}), bf16[256,2048]{1,0:T(8,128)(2,1)}) %reduce-scatter.13.cloned.1.call-update) | async-done | bytes 1048592 | tf_op jit(solution)/shard_map/reduce_scatter | solution.py:286
  705.7 3.4 fusion.108
  712.1 11.0 fusion.25
  724.7 9.4 convolution_convert_fusion.5
  734.5 31.9 %all-gather.29.cloned.1.call-done = bf16[2048,2048]{1,0:T(8,128)(2,1)} async-done(((bf16[256,2048]{1,0:T(8,128)(2,1)}), bf16[2048,2048]{1,0:T(8,128)(2,1)}) %all-gather.29.cloned.1.call-update) | async-done | bytes 8388624 | tf_op jit(solution)/shard_map/all_gather | solution.py:283
  766.4 14.2 %multiply_reduce_fusion = (f32[2048]{0:T(1024)S(1)}, f32[2048,512]{1,0:T(8,128)S(1)}) fusion(f32[8,1,512,256]{2,3,0,1:T(8,128)} %copy-done.2, f32[2048]{0:T(1024)S(1)} %bitcast.278, f32[2048,512]{1,0:T(8,128)} %get-tuple-element.77, bf16[2048,2048]{1,0:T(8,128)(2,1)} %all-gather.29.cloned.1.call-done, bf16[2048,512]{1,0:T(8,128)(2,1)S(1)} %copy-done.50), kind=kOutput, calls=%fused_computation.36 | convolution fusion | flops 4303353856 | bytes 23085056 | tf_op jit(solution)/shard_map/dot_general | solution.py:366
  780.6 4.9 fusion.107
  794.6 4.2 fusion.94
  803.1 2.6 copy.131
  805.6 2.6 copy.130
  809.0 2.2 fusion.88
  811.9 4.1 fusion.37
  817.4 2.5 copy.133
  820.0 2.6 copy.132
  822.6 5.8 fusion.79
  830.5 10.2 convolution_convert_fusion.8
  840.8 9.9 convolution_convert_fusion.4
  850.8 9.9 convolution_convert_fusion.6
  860.8 6.1 fusion.10
  869.1 9.4 convolution_convert_fusion.7
  880.1 10.0 fusion.68
  890.2 8.4 fusion.117
  898.6 17.4 %add_convert_fusion = bf16[2048,2048]{1,0:T(8,128)(2,1)} fusion(f32[2048,2048]{1,0:T(8,128)} %fusion.68, f32[2048,2048]{1,0:T(8,128)} %fusion.117, bf16[2048,512]{1,0:T(8,128)(2,1)S(1)} %copy-done.11, bf16[2048,512]{1,0:T(8,128)(2,1)} %all-gather.13.cloned.1.call-done), kind=kOutput, calls=%fused_computation | convolution fusion | flops 4307550208 | bytes 46137344 | tf_op jit(solution)/shard_map/dot_general | solution.py:103
  918.1 3.7 all-to-all-start.6
  921.9 9.6 all-to-all-done.6
  931.5 3.5 all-to-all-start.4
  936.8 7.9 all-to-all-done.4
  944.7 9.3 all_to_all.91
  954.0 3.4 all-to-all-start.1
  957.5 6.8 all-to-all-done.1
  964.3 3.5 all-to-all-start.5
  967.8 26.4 %reduce-scatter.23.cloned.1.call-done = bf16[512,512]{1,0:T(8,128)(2,1)} async-done(((bf16[2048,512]{1,0:T(8,128)(2,1)}), bf16[512,512]{1,0:T(8,128)(2,1)}) %reduce-scatter.23.cloned.1.call-update) | async-done | bytes 524304 | tf_op jit(solution)/shard_map/reduce_scatter | solution.py:347
  994.2 3.7 all-to-all-start.3
  998.0 41.7 %reduce-scatter.21.cloned.1.call-done = bf16[512,512]{1,0:T(8,128)(2,1)} async-done(((bf16[2048,512]{1,0:T(8,128)(2,1)}), bf16[512,512]{1,0:T(8,128)(2,1)}) %reduce-scatter.21.cloned.1.call-update) | async-done | bytes 524304 | tf_op jit(solution)/shard_map/reduce_scatter | solution.py:347
  1039.7 3.7 all-to-all-start.2
  1045.0 8.2 all-to-all-done.2
  1057.5 5.3 concatenate.33
  1062.8 51.3 %reduce-scatter.17.cloned.1.call-done = bf16[256,2048]{1,0:T(8,128)(2,1)} async-done(((bf16[2048,2048]{1,0:T(8,128)(2,1)}), bf16[256,2048]{1,0:T(8,128)(2,1)}) %reduce-scatter.17.cloned.1.call-update) | async-done | bytes 1048592 | tf_op jit(solution)/shard_map/reduce_scatter | solution.py:286
  1116.0 2.3 fusion.36
  1118.4 40.1 %all-reduce.4 = (f32[2,2048]{1,0:T(2,128)}, f32[2,2048]{1,0:T(2,128)}) all-reduce(f32[2,2048]{1,0:T(2,128)S(1)} %pad_maximum_fusion.6, f32[2,2048]{1,0:T(2,128)S(1)} %pad_maximum_fusion.7), channel_id=1, replica_groups=mesh['dp'=4,'seq'=8] {'dp','seq'}, use_global_device_ids=true, to_apply=%region_25.26 | all-reduce | flops 8192 | bytes 65536 | tf_op jit(solution)/shard_map/psum | solution.py:432
  1158.5 3.8 add_add_fusion.3
  (249 shorter events, 72.2 us)
Async XLA Ops:
  7.2 2.2 copy-start
  7.2 51.1 %all-gather.17.cloned.1.call-start = ((), (), s32[]{:S(2)}) async-start(), calls=%async_computation.20 | async-start | bytes 2621440 | tf_op jit(solution)/shard_map/all_gather | solution.py:273
  9.3 104.9 %all-gather.11.cloned.1.call-start = ((), (), s32[]{:S(2)}) async-start(), calls=%async_computation.17 | async-start | bytes 9437184 | tf_op jit(solution)/shard_map/all_gather | solution.py:283
  10.0 5.4 copy-start.44
  10.0 5.4 copy-start.38
  12.1 150.1 %all-gather.15.cloned.1.call-start = ((), (), s32[]{:S(2)}) async-start(), calls=%async_computation.19 | async-start | bytes 2621440 | tf_op jit(solution)/shard_map/all_gather | solution.py:273
  12.2 4.6 copy-start.48
  15.4 192.8 %all-gather.13.cloned.1.call-start = ((), (), s32[]{:S(2)}) async-start(), calls=%async_computation.18 | async-start | bytes 2621440 | tf_op jit(solution)/shard_map/all_gather | solution.py:273
  16.0 238.3 %all-gather.19.cloned.1.call-start = ((), (), s32[]{:S(2)}) async-start(), calls=%async_computation.21 | async-start | bytes 2621440 | tf_op jit(solution)/shard_map/all_gather | solution.py:273
  16.6 316.2 %reduce-scatter.11.cloned.1.call-start = ((), (), s32[]{:S(2)}) async-start(), calls=%async_computation.22 | async-start | bytes 9437184 | tf_op jit(solution)/shard_map/reduce_scatter | solution.py:286
  16.7 105.4 %copy-start.46 = (f32[128]{0:T(128)}, f32[128]{0:T(128)S(1)}, u32[]{:S(2)}) copy-start(f32[128]{0:T(128)S(1)} %negate_power_fusion) | copy-start | bytes 1540
  16.7 105.4 %copy-start.32 = (f32[2048]{0:T(1024)}, f32[2048]{0:T(1024)S(1)}, u32[]{:S(2)}) copy-start(f32[2048]{0:T(1024)S(1)} %iota_convert_fusion) | copy-start | bytes 24580
  128.3 54.0 %copy-start.14 = (bf16[32,8,8,256]{3,2,1,0:T(8,128)(2,1)}, bf16[32,8,8,256]{3,2,1,0:T(8,128)(2,1)S(1)}, u32[]{:S(2)}) copy-start(bf16[32,8,8,256]{3,2,1,0:T(8,128)(2,1)S(1)} %copy.141) | copy-start | bytes 3145732
  130.2 43.1 %copy-start.12 = (bf16[2048,1,256]{2,0,1:T(8,128)(2,1)}, bf16[2048,1,256]{2,0,1:T(8,128)(2,1)S(1)}, u32[]{:S(2)}) copy-start(bf16[2048,1,256]{2,0,1:T(8,128)(2,1)S(1)} %copy.129) | copy-start | bytes 3145732
  170.8 3.8 copy-start.9
  174.6 2.0 copy-start.16
  182.3 1.8 copy-start.17
  184.1 2.0 copy-start.2
  218.3 44.3 %copy-start.52 = (bf16[2048,512]{1,0:T(8,128)(2,1)}, bf16[2048,512]{1,0:T(8,128)(2,1)S(1)}, u32[]{:S(2)}) copy-start(bf16[2048,512]{1,0:T(8,128)(2,1)S(1)} %get-tuple-element.76) | copy-start | bytes 6291460
  262.7 117.7 %all-gather.23.cloned.1.call-start = ((), (), s32[]{:S(2)}) async-start(), calls=%async_computation.24 | async-start | bytes 2621440 | tf_op jit(solution)/shard_map/all_gather | solution.py:273
  263.4 172.7 %all-gather.21.cloned.1.call-start = ((), (), s32[]{:S(2)}) async-start(), calls=%async_computation.23 | async-start | bytes 9437184 | tf_op jit(solution)/shard_map/all_gather | solution.py:283
  336.6 147.2 %all-gather.25.cloned.1.call-start = ((), (), s32[]{:S(2)}) async-start(), calls=%async_computation.25 | async-start | bytes 2621440 | tf_op jit(solution)/shard_map/all_gather | solution.py:273
  337.3 201.5 %all-gather.27.cloned.1.call-start = ((), (), s32[]{:S(2)}) async-start(), calls=%async_computation.27 | async-start | bytes 9437184 | tf_op jit(solution)/shard_map/all_gather | solution.py:283
  337.9 293.2 %reduce-scatter.15.cloned.1.call-start = ((), (), s32[]{:S(2)}) async-start(), calls=%async_computation.28 | async-start | bytes 9437184 | tf_op jit(solution)/shard_map/reduce_scatter | solution.py:286
  538.8 13.7 %copy-start.51 = (bf16[2048,512]{1,0:T(8,128)(2,1)S(1)}, bf16[2048,512]{1,0:T(8,128)(2,1)}, u32[]{:S(2)}) copy-start(bf16[2048,512]{1,0:T(8,128)(2,1)} %all-gather.23.cloned.1.call-done) | copy-start | bytes 6291460
  559.6 146.1 %reduce-scatter.13.cloned.1.call-start = ((), (), s32[]{:S(2)}) async-start(), calls=%async_computation.26 | async-start | bytes 9437184 | tf_op jit(solution)/shard_map/reduce_scatter | solution.py:286
  572.1 194.3 %all-gather.29.cloned.1.call-start = ((), (), s32[]{:S(2)}) async-start(), calls=%async_computation.29 | async-start | bytes 9437184 | tf_op jit(solution)/shard_map/all_gather | solution.py:283
  633.8 76.7 %copy-start.19 = (bf16[256,2048]{1,0:T(8,128)(2,1)S(1)}, bf16[256,2048]{1,0:T(8,128)(2,1)}, u32[]{:S(2)}) copy-start(bf16[256,2048]{1,0:T(8,128)(2,1)} %param.11) | copy-start | bytes 3145732
  709.1 2.7 copy-start.42
  711.9 204.1 %reduce-scatter.29.cloned.1.call-start = ((), (), s32[]{:S(2)}) async-start(), calls=%async_computation.36 | async-start | bytes 2621440 | tf_op jit(solution)/shard_map/reduce_scatter | solution.py:347
  723.2 198.7 %reduce-scatter.25.cloned.1.call-start = ((), (), s32[]{:S(2)}) async-start(), calls=%async_computation.34 | async-start | bytes 2621440 | tf_op jit(solution)/shard_map/reduce_scatter | solution.py:347
  734.2 32.2 %copy-start.50 = (bf16[2048,512]{1,0:T(8,128)(2,1)S(1)}, bf16[2048,512]{1,0:T(8,128)(2,1)}, u32[]{:S(2)}) copy-start(bf16[2048,512]{1,0:T(8,128)(2,1)} %all-gather.19.cloned.1.call-done) | copy-start | bytes 6291460
  734.2 200.8 %reduce-scatter.19.cloned.1.call-start = ((), (), s32[]{:S(2)}) async-start(), calls=%async_computation.31 | async-start | bytes 2621440 | tf_op jit(solution)/shard_map/reduce_scatter | solution.py:347
  766.4 14.2 %copy-start.3 = (f32[8,1,512,256]{2,3,0,1:T(8,128)S(1)}, f32[8,1,512,256]{2,3,0,1:T(8,128)}, u32[]{:S(2)}) copy-start(f32[8,1,512,256]{2,3,0,1:T(8,128)} %copy-done.2) | copy-start | bytes 12582916
  766.4 14.2 %copy-start.22 = (f32[2048,512]{1,0:T(8,128)S(1)}, f32[2048,512]{1,0:T(8,128)}, u32[]{:S(2)}) copy-start(f32[2048,512]{1,0:T(8,128)} %get-tuple-element.77) | copy-start | bytes 12582916
  788.7 2.0 copy-start.23
  788.7 2.0 copy-start.13
  801.0 2.0 copy-start.5
  809.0 2.9 copy-start.6
  817.4 5.1 copy-start.33
  817.4 5.1 copy-start.47
  840.8 116.7 %reduce-scatter.27.cloned.1.call-start = ((), (), s32[]{:S(2)}) async-start(), calls=%async_computation.35 | async-start | bytes 2621440 | tf_op jit(solution)/shard_map/reduce_scatter | solution.py:347
  850.8 143.4 %reduce-scatter.23.cloned.1.call-start = ((), (), s32[]{:S(2)}) async-start(), calls=%async_computation.33 | async-start | bytes 2621440 | tf_op jit(solution)/shard_map/reduce_scatter | solution.py:347
  860.8 178.9 %reduce-scatter.21.cloned.1.call-start = ((), (), s32[]{:S(2)}) async-start(), calls=%async_computation.32 | async-start | bytes 2621440 | tf_op jit(solution)/shard_map/reduce_scatter | solution.py:347
  860.8 6.2 copy-start.21
  878.6 235.5 %reduce-scatter.17.cloned.1.call-start = ((), (), s32[]{:S(2)}) async-start(), calls=%async_computation.30 | async-start | bytes 9437184 | tf_op jit(solution)/shard_map/reduce_scatter | solution.py:286
  880.1 10.0 copy-start.25
  880.1 10.0 copy-start.49
  890.2 8.4 copy-start.11
  918.1 13.4 %all-to-all-start.6 = ((bf16[8,64,512]{2,1,0:T(8,128)(2,1)}), bf16[8,64,512]{2,1,0:T(8,128)(2,1)S(1)}, u32[]{:S(2)}, u32[]{:S(2)}) async-start(bf16[8,64,512]{2,1,0:T(8,128)(2,1)} %bitcast.70), calls=%async_computation.16 | async-start | bytes 1048576 | tf_op jit(solution)/shard_map/all_to_all | solution.py:355
  931.5 13.2 %all-to-all-start.4 = ((bf16[8,64,512]{2,1,0:T(8,128)(2,1)}), bf16[8,64,512]{2,1,0:T(8,128)(2,1)S(1)}, u32[]{:S(2)}, u32[]{:S(2)}) async-start(bf16[8,64,512]{2,1,0:T(8,128)(2,1)} %bitcast.264), calls=%async_computation.12 | async-start | bytes 1048576 | tf_op jit(solution)/shard_map/all_to_all | solution.py:355
  954.0 10.3 all-to-all-start.1
  964.3 29.9 %all-to-all-start.5 = ((bf16[8,64,512]{2,1,0:T(8,128)(2,1)}), bf16[8,64,512]{2,1,0:T(8,128)(2,1)S(1)}, u32[]{:S(2)}, u32[]{:S(2)}) async-start(bf16[8,64,512]{2,1,0:T(8,128)(2,1)} %bitcast.267), calls=%async_computation.14 | async-start | bytes 1048576 | tf_op jit(solution)/shard_map/all_to_all | solution.py:355
  994.2 45.5 %all-to-all-start.3 = ((bf16[8,64,512]{2,1,0:T(8,128)(2,1)}), bf16[8,64,512]{2,1,0:T(8,128)(2,1)S(1)}, u32[]{:S(2)}, u32[]{:S(2)}) async-start(bf16[8,64,512]{2,1,0:T(8,128)(2,1)} %bitcast.265), calls=%async_computation.10 | async-start | bytes 1048576 | tf_op jit(solution)/shard_map/all_to_all | solution.py:355
  1039.7 13.4 %all-to-all-start.2 = ((bf16[8,64,512]{2,1,0:T(8,128)(2,1)}), bf16[8,64,512]{2,1,0:T(8,128)(2,1)S(1)}, u32[]{:S(2)}, u32[]{:S(2)}) async-start(bf16[8,64,512]{2,1,0:T(8,128)(2,1)} %bitcast.266), calls=%async_computation.8 | async-start | bytes 1048576 | tf_op jit(solution)/shard_map/all_to_all | solution.py:355
  1057.5 56.6 %copy-start.1 = (bf16[256,2048]{1,0:T(8,128)(2,1)S(1)}, bf16[256,2048]{1,0:T(8,128)(2,1)}, u32[]{:S(2)}) copy-start(bf16[256,2048]{1,0:T(8,128)(2,1)} %param.6) | copy-start | bytes 3145732
  1057.5 56.6 %copy-start.31 = (f32[1,2048]{1,0:T(1,128)S(1)}, f32[1,2048]{1,0:T(1,128)}, u32[]{:S(2)}) copy-start(f32[1,2048]{1,0:T(1,128)} %copy-done.30) | copy-start | bytes 24580
  1057.5 56.6 %copy-start.35 = (f32[256]{0:T(256)S(1)}, f32[256]{0:T(256)}, u32[]{:S(2)}) copy-start(f32[256]{0:T(256)} %copy-done.34) | copy-start | bytes 3076
  1062.7 53.3 %copy-start.45 = (f32[256]{0:T(256)S(1)}, f32[256]{0:T(256)}, u32[]{:S(2)}) copy-start(f32[256]{0:T(256)} %copy-done.44) | copy-start | bytes 3076
  1062.7 53.3 %copy-start.39 = (f32[256]{0:T(256)S(1)}, f32[256]{0:T(256)}, u32[]{:S(2)}) copy-start(f32[256]{0:T(256)} %copy-done.38) | copy-start | bytes 3076
  1062.7 55.6 %copy-start.37 = (f32[2048]{0:T(1024)S(1)}, f32[2048]{0:T(1024)}, u32[]{:S(2)}) copy-start(f32[2048]{0:T(1024)} %get-tuple-element.11) | copy-start | bytes 24580
  1062.7 55.6 %copy-start.36 = (f32[2048]{0:T(1024)S(1)}, f32[2048]{0:T(1024)}, u32[]{:S(2)}) copy-start(f32[2048]{0:T(1024)} %get-tuple-element.5) | copy-start | bytes 24580
  1062.7 95.8 %copy-start.8 = (f32[256,2048]{1,0:T(8,128)S(1)}, f32[256,2048]{1,0:T(8,128)}, u32[]{:S(2)}) copy-start(f32[256,2048]{1,0:T(8,128)} %copy-done.7) | copy-start | bytes 6291460
  1062.8 95.8 %copy-start.43 = (f32[256]{0:T(256)S(1)}, f32[256]{0:T(256)}, u32[]{:S(2)}) copy-start(f32[256]{0:T(256)} %copy-done.42) | copy-start | bytes 3076
  (17 other events, 22.3 us)
Sparse Core Ops, SparseCore 0:
  9.6 48.6 all-gather.16
  60.7 53.3 all-gather.10
  116.3 45.9 all-gather.14
  163.7 44.5 all-gather.12
  209.7 44.6 all-gather.18
  262.8 69.9 reduce-scatter.10
  334.5 45.9 all-gather.22
  383.0 53.0 all-gather.20
  437.8 45.9 all-gather.24
  485.7 53.0 all-gather.26
  559.7 71.3 reduce-scatter.14
  634.4 71.2 reduce-scatter.12
  712.0 54.3 all-gather.28
  768.6 43.8 reduce-scatter.28
  814.7 43.1 reduce-scatter.24
  860.2 43.1 reduce-scatter.18
  905.5 43.1 reduce-scatter.26
  951.0 43.1 reduce-scatter.22
  996.5 43.1 reduce-scatter.20
  1043.4 70.6 reduce-scatter.16

commit v2 on v1

--- a/solution.py
+++ b/solution.py
@@ -1,6 +1,10 @@
+import functools
+
 import jax
 import jax.numpy as jnp
 from jax import lax
+from jax.experimental import pallas as pl
+from jax.experimental.pallas import tpu as pltpu
 from jax.sharding import PartitionSpec as P
 
 HEADS = 8
@@ -246,6 +250,380 @@
     return (result, grad_tokens, grad_weights, grad_gain, grad_bias)
 
 
+MESH = pl.DeviceIdType.MESH
+ANY = pl.BlockSpec(memory_space=pl.ANY)
+DMA = pltpu.SemaphoreType.DMA
+
+
+def cost(flops, moved):
+    return pl.CostEstimate(flops=int(flops), bytes_accessed=int(moved), transcendentals=0)
+
+
+def flipped(index, size):
+    return index + size * (1 - 2 * ((index // size) % 2))
+
+
+def row_peers():
+    me = lax.axis_index("seq")
+    return me, flipped(me, 1), flipped(me, 2), flipped(me, 4)
+
+
+def greet(others):
+    barrier = pltpu.get_barrier_semaphore()
+    for axis, other in others:
+        pl.semaphore_signal(barrier, inc=1, device_id={axis: other}, device_id_type=MESH)
+    pl.semaphore_wait(barrier, len(others))
+
+
+def seq_copy(src, dst, send, recv, target):
+    return pltpu.make_async_remote_copy(
+        src_ref=src,
+        dst_ref=dst,
+        send_sem=send,
+        recv_sem=recv,
+        device_id={"seq": target},
+        device_id_type=MESH,
+    )
+
+
+def gather_kernel(chunks, own, out, send, recv, local):
+    me, core, along, across = row_peers()
+    corner = along + across - me
+    rows = own.shape[0] // chunks
+    half = chunks // 2
+    greet([("seq", core), ("seq", along), ("seq", across)])
+
+    def copy(lane, k, who, target):
+        part = pl.ds(k * rows, rows)
+        src = own.at[part] if lane in (0, 1, 4) else out.at[who, part]
+        return seq_copy(src, out.at[who, part], send.at[lane, k], recv.at[lane, k], target)
+
+    mine = pltpu.make_async_copy(own, out.at[me], local)
+    mine.start()
+    started = []
+
+    def go(one):
+        one.start()
+        started.append(one)
+
+    order_along = list(range(chunks))
+    order_across = order_along[half:] + order_along[:half]
+    for i in range(chunks):
+        go(copy(0, order_along[i], me, along))
+        go(copy(1, order_across[i], me, across))
+        go(copy(4, order_along[i], me, core))
+    for i in range(chunks):
+        k = order_along[i]
+        copy(0, k, along, along).wait_recv()
+        if k < half:
+            go(copy(3, k, along, across))
+        go(copy(5, k, along, core))
+        k = order_across[i]
+        copy(1, k, across, across).wait_recv()
+        if k >= half:
+            go(copy(2, k, across, along))
+        go(copy(6, k, across, core))
+    for k in range(half):
+        copy(3, k, corner, across).wait_recv()
+        go(copy(7, k, corner, core))
+        copy(2, half + k, corner, along).wait_recv()
+        go(copy(7, half + k, corner, core))
+    turn = core - me
+    for k in range(chunks):
+        copy(4, k, core, core).wait_recv()
+        copy(5, k, along + turn, core).wait_recv()
+        copy(6, k, across + turn, core).wait_recv()
+        copy(7, k, corner + turn, core).wait_recv()
+    for one in started:
+        one.wait_send()
+    mine.wait()
+
+
+def row_gather(own, ident, chunks=8):
+    shape = (8,) + own.shape
+    out = pl.pallas_call(
+        functools.partial(gather_kernel, chunks),
+        out_shape=jax.ShapeDtypeStruct(shape, own.dtype),
+        in_specs=[ANY],
+        out_specs=ANY,
+        scratch_shapes=[DMA((8, chunks)), DMA((8, chunks)), DMA],
+        compiler_params=pltpu.CompilerParams(collective_id=ident, has_side_effects=True),
+        cost_estimate=cost(0, 120e6),
+        name=f"row_gather_{ident}",
+    )(own)
+    return out.reshape((8 * own.shape[0],) + own.shape[1:])
+
+
+def scatter_kernel(tile, exact, left, right, *refs):
+    if exact:
+        few, out, few_out, *refs, few_recv, few_sems = refs
+    else:
+        out, *refs = refs
+    core_send, core_recv, far_send, far_recv, near_send, near_recv, wide, *refs = refs
+    core_sems, far_sems, near_sems = refs
+    me, core, along, across = row_peers()
+    corner = along + across - me
+    turn = core - me
+    rows = out.shape[0]
+    half = rows // 2
+    tiles = out.shape[1] // tile
+    greet([("seq", core), ("seq", along), ("seq", across)])
+    halves = (pl.ds(0, half), pl.ds(half, half))
+
+    def few_copy(i):
+        return seq_copy(
+            few_out, few_recv.at[i], few_sems.at[0, i], few_sems.at[1, i], (core, along, across)[i]
+        )
+
+    def few_step(i):
+        if exact:
+            few_copy(i).wait()
+            few_out[...] += few_recv[i]
+            if i < 2:
+                few_copy(i + 1).start()
+
+    def product(block, sink):
+        at = pl.ds(pl.multiple_of(block * rows, rows), rows)
+
+        @pl.loop(0, tiles)
+        def _(i):
+            cols = pl.ds(pl.multiple_of(i * tile, tile), tile)
+            sink(cols, contract_last(left[at, :], right[cols, :]))
+
+    def core_copy(i):
+        return seq_copy(
+            core_send.at[i], core_recv.at[i], core_sems.at[0, i], core_sems.at[1, i], core
+        )
+
+    def far_copy(i):
+        return seq_copy(
+            far_send.at[halves[i]],
+            far_recv.at[halves[i]],
+            far_sems.at[0, i],
+            far_sems.at[1, i],
+            (along, across)[i],
+        )
+
+    def near_copy(i, part):
+        return seq_copy(
+            near_send.at[i, halves[part]],
+            near_recv.at[i, halves[part]],
+            near_sems.at[0, 2 * i + part],
+            near_sems.at[1, 2 * i + part],
+            (along, across)[i],
+        )
+
+    def for_core(i, block):
+        def sink(cols, value):
+            core_send[i, :, cols] = value.astype(bf16)
+
+        product(block, sink)
+        core_copy(i).start()
+
+    def near(i, block):
+        core_copy(1 + i).wait_recv()
+        ready, late = (0, 1) if i == 0 else (1, 0)
+
+        def sink(cols, value):
+            total = value + core_recv[1 + i, :, cols].astype(f32)
+            near_send[i, halves[ready], cols] = total[ready * half : (ready + 1) * half].astype(bf16)
+            wide[i, :, cols] = total[late * half : (late + 1) * half]
+
+        product(block, sink)
+        near_copy(i, ready).start()
+
+    def near_late(i):
+        late = 1 if i == 0 else 0
+        far_copy(late).wait_recv()
+
+        @pl.loop(0, tiles)
+        def _(t):
+            cols = pl.ds(pl.multiple_of(t * tile, tile), tile)
+            total = wide[i, :, cols] + far_recv[halves[late], cols].astype(f32)
+            near_send[i, halves[late], cols] = total.astype(bf16)
+
+        near_copy(i, late).start()
+
+    if exact:
+
+        @pl.loop(0, tiles)
+        def _(i):
+            cols = pl.ds(pl.multiple_of(i * tile, tile), tile)
+            few_out[:, cols] = contract_last(few[...], right[cols, :])
+
+        few_copy(0).start()
+
+    for_core(0, corner + turn)
+    for_core(1, along + turn)
+    core_copy(0).wait_recv()
+
+    def far_sink(cols, value):
+        far_send[:, cols] = (value + core_recv[0, :, cols].astype(f32)).astype(bf16)
+
+    product(corner, far_sink)
+    far_copy(0).start()
+    far_copy(1).start()
+    for_core(2, across + turn)
+    few_step(0)
+    near(0, along)
+    few_step(1)
+    near(1, across)
+    few_step(2)
+    for_core(3, core)
+    core_copy(3).wait_recv()
+
+    def own_sink(cols, value):
+        out[:, cols] = value + core_recv[3, :, cols].astype(f32)
+
+    product(me, own_sink)
+    near_late(0)
+    near_late(1)
+    for part, i in ((0, 0), (1, 1), (1, 0), (0, 1)):
+        near_copy(i, part).wait_recv()
+
+        @pl.loop(0, tiles)
+        def _(t):
+            cols = pl.ds(pl.multiple_of(t * tile, tile), tile)
+            out[halves[part], cols] += near_recv[i, halves[part], cols].astype(f32)
+
+    for i in range(4):
+        core_copy(i).wait_send()
+    for i in range(2):
+        far_copy(i).wait_send()
+        near_copy(i, 0).wait_send()
+        near_copy(i, 1).wait_send()
+
+
+def row_scatter(left, right, ident, column=0, tile=512, few=None):
+    depth = left.shape[1]
+    rows, width = left.shape[0] // 8, right.shape[0]
+    whole = pltpu.VMEM
+    exact = few is not None
+    extra_in, extra_out, extra_scratch = [], [], []
+    shapes = [jax.ShapeDtypeStruct((rows, width), f32)]
+    if exact:
+        count = few.shape[0]
+        extra_in = [pl.BlockSpec((count, depth), lambda i: (0, 0))]
+        extra_out = [pl.BlockSpec((count, width), lambda i: (0, 0))]
+        extra_scratch = [whole((3, count, width), f32), DMA((2, 3))]
+        shapes.append(jax.ShapeDtypeStruct((count, width), f32))
+    out = pl.pallas_call(
+        functools.partial(scatter_kernel, tile, exact),
+        out_shape=shapes,
+        grid=(1,),
+        in_specs=[
+            pl.BlockSpec((8 * rows, depth), lambda i: (0, 0), pipeline_mode=pl.Buffered(1)),
+            pl.BlockSpec((width, depth), lambda i: (0, column), pipeline_mode=pl.Buffered(1)),
+        ]
+        + extra_in,
+        out_specs=[pl.BlockSpec((rows, width), lambda i: (0, 0), pipeline_mode=pl.Buffered(1))]
+        + extra_out,
+        scratch_shapes=[
+            whole((4, rows, width), bf16),
+            whole((4, rows, width), bf16),
+            whole((rows, width), bf16),
+            whole((rows, width), bf16),
+            whole((2, rows, width), bf16),
+            whole((2, rows, width), bf16),
+            whole((2, rows // 2, width), f32),
+            DMA((2, 4)),
+            DMA((2, 2)),
+            DMA((2, 4)),
+        ]
+        + extra_scratch,
+        compiler_params=pltpu.CompilerParams(
+            collective_id=ident, has_side_effects=True, vmem_limit_bytes=48 * 2**20
+        ),
+        cost_estimate=cost(16 * rows * depth * width, 120e6),
+        name=f"row_scatter_{ident}",
+    )(*([left, right] + ([few] if exact else [])))
+    return out if exact else out[0]
+
+
+def exchange_kernel(widths, grad, *refs):
+    outs, (send, recv, local) = refs[: len(widths)], refs[len(widths) :]
+    me = lax.axis_index("seq")
+    rows = outs[0].shape[0]
+    others = []
+    for step in range(8):
+        other = me
+        for size in (1, 2, 4):
+            if step & size:
+                other = flipped(other, size)
+        others.append(other)
+    greet([("seq", other) for other in others[1:]])
+    started = []
+    for step in (6, 7, 2, 3, 4, 5, 1, 0):
+        other = others[step]
+        at = pl.ds(pl.multiple_of(other * rows, rows), rows)
+        start = 0
+        for i, width in enumerate(widths):
+            src = grad.at[at, pl.ds(start, width)]
+            dst = outs[i].at[:, pl.ds(pl.multiple_of(me * width, width), width)]
+            start += width
+            if step == 0:
+                one = pltpu.make_async_copy(src, dst, local.at[i])
+            else:
+                one = seq_copy(src, dst, send.at[step, i], recv.at[step, i], other)
+            one.start()
+            started.append(one)
+    for one in started:
+        one.wait()
+
+
+def row_exchange(grad, widths, ident):
+    rows = grad.shape[0] // 8
+    n = len(widths)
+    return pl.pallas_call(
+        functools.partial(exchange_kernel, widths),
+        out_shape=[jax.ShapeDtypeStruct((rows, 8 * width), grad.dtype) for width in widths],
+        in_specs=[ANY],
+        out_specs=[ANY] * n,
+        scratch_shapes=[DMA((8, n)), DMA((8, n)), DMA((n,))],
+        compiler_params=pltpu.CompilerParams(collective_id=ident, has_side_effects=True),
+        cost_estimate=cost(0, 30e6),
+        name=f"row_exchange_{ident}",
+    )(grad)
+
+
+def total_kernel(stages, own, out, held, send, recv):
+    places = {axis: lax.axis_index(axis) for axis, _ in stages}
+    partners = [(axis, flipped(places[axis], size)) for axis, size in stages]
+    greet(partners)
+    out[...] = own[...]
+    for i, (axis, other) in enumerate(partners):
+        copy = pltpu.make_async_remote_copy(
+            src_ref=out,
+            dst_ref=held.at[i],
+            send_sem=send.at[i],
+            recv_sem=recv.at[i],
+            device_id={axis: other},
+            device_id_type=MESH,
+        )
+        copy.start()
+        copy.wait()
+        out[...] += held[i]
+
+
+def device_total(own, dp_size, ident):
+    stages = [("seq", 1), ("seq", 2), ("seq", 4)]
+    size = 1
+    while size < dp_size:
+        stages.append(("dp", size))
+        size *= 2
+    n = len(stages)
+    return pl.pallas_call(
+        functools.partial(total_kernel, stages),
+        out_shape=jax.ShapeDtypeStruct(own.shape, f32),
+        in_specs=[pl.BlockSpec(memory_space=pltpu.VMEM)],
+        out_specs=pl.BlockSpec(memory_space=pltpu.VMEM),
+        scratch_shapes=[pltpu.VMEM((n,) + own.shape, f32), DMA((n,)), DMA((n,))],
+        compiler_params=pltpu.CompilerParams(collective_id=ident, has_side_effects=True),
+        cost_estimate=cost(0, 30e6),
+        name=f"device_total_{ident}",
+    )(own)
+
+
 def sections(n_seq):
     widths = (HEADS * QK, HEADS * QK, HEADS * VD, HEADS * VD, FF, HEADS * VD, FF)
     start, out = 0, []
@@ -272,20 +650,12 @@
         )
         return lax.all_gather(part, "dp", axis=0, tiled=True)
 
-    w_qk = gather_weights((0, 1))
-    w_v = gather_weights((2,))
-    w_g = gather_weights((3,))
+    mix = gather_weights((0, 1, 2, 3))
     w_out = gather_weights((5,))
-    w_in = gather_weights((4,))
-    w_down = gather_weights((6,))
-
-    def row_gather(part):
-        return lax.all_gather(part, "seq", axis=0, tiled=True)
-
-    def row_scatter(full):
-        return lax.psum_scatter(
-            full.astype(bf16), "seq", scatter_dimension=0, tiled=True
-        ).astype(f32)
+    ffn = gather_weights((4, 6))
+    ffn_width = FF // n_seq
+    q_end, k_end = heads * QK, 2 * heads * QK
+    v_end = k_end + heads * VD
 
     positions = jnp.arange(length, dtype=jnp.int32)
     starts = doc_starts[0]
@@ -294,22 +664,22 @@
     seg_before = jnp.concatenate([jnp.zeros((1,), jnp.int32), seg_blocks[:-1, -1]])
     inputs = tokens.astype(f32)
     first, first_pull = jax.vjp(layer_norm, inputs, ln_gain[0], ln_bias[0])
-    first_low = row_gather(first.astype(bf16))
-    cot_low = row_gather(cotangent)
-    qk_raw = jnp.dot(first_low, w_qk, preferred_element_type=f32)
+    first_low = row_gather(first.astype(bf16), 1)
+    cot_low = row_gather(cotangent, 2)
+    project = jnp.dot(first_low, mix, preferred_element_type=f32)
 
     def rotate_here(values):
         return rotate(values, positions, heads)
 
-    query_rot, rotate_pull = jax.vjp(rotate_here, qk_raw[:, : heads * QK])
+    query_rot, rotate_pull = jax.vjp(rotate_here, project[:, :q_end])
 
     def blocked(values):
         return values.reshape(n_seq, block, heads, -1)
 
     query_low = blocked(query_rot.astype(bf16))
-    key_low = blocked(rotate_here(qk_raw[:, heads * QK :]).astype(bf16))
-    value_low = blocked(jnp.dot(first_low, w_v, preferred_element_type=f32).astype(bf16))
-    gate_raw = jnp.dot(first_low, w_g, preferred_element_type=f32)
+    key_low = blocked(rotate_here(project[:, q_end:k_end]).astype(bf16))
+    value_low = blocked(project[:, k_end:v_end].astype(bf16))
+    gate_raw = project[:, v_end:]
     logs = lax.dynamic_slice_in_dim(head_logs(), place * heads, heads)
     within, reach, ending, carry = jax.vmap(decay_tables, (0, 0, None))(
         seg_blocks, seg_before, logs
@@ -334,39 +704,63 @@
     grouped, group_pull = jax.vjp(group_norm, mixed)
     gated, gating_pull = jax.vjp(gating, gate_raw, grouped.reshape(length, heads * VD))
     gated_low = gated.astype(bf16)
-    hidden = inputs + row_scatter(contract_last(gated_low, w_out))
+    local = place * block + jnp.arange(block, dtype=jnp.int32)
+    some = jnp.tile(starts, 4)
+    picks = (some[:, None] == positions[None, :]).astype(bf16)
+
+    def few_rows(values):
+        return jnp.dot(picks, values, preferred_element_type=f32).astype(bf16)
+
+    def exact_scatter(left, right, ident):
+        out, few = row_scatter(left, right, ident, few=few_rows(left))
+        for i in range(starts.shape[0]):
+            out = jnp.where((local == starts[i])[:, None], few[i][None, :], out)
+        return out
+
+    hidden = inputs + exact_scatter(gated_low, w_out, 3)
     second, second_pull = jax.vjp(layer_norm, hidden, ln_gain[1], ln_bias[1])
-    second_low = row_gather(second.astype(bf16))
-    inner = jnp.dot(second_low, w_in, preferred_element_type=f32)
+    second_low = row_gather(second.astype(bf16), 4)
+    inner = jnp.dot(second_low, ffn[:, :ffn_width], preferred_element_type=f32)
     active, active_pull = jax.vjp(gelu_tanh, inner)
     active_low = active.astype(bf16)
-    result = (hidden + row_scatter(contract_last(active_low, w_down))).astype(bf16)
     contract = (((0,), (0,)), ((), ()))
 
-    def weight_grad(left, right):
+    def product(left, right):
+        return lax.dot_general(left, right, contract, preferred_element_type=f32).astype(bf16)
+
+    def reduce_dp(grads):
         return lax.psum_scatter(
-            lax.dot_general(left, right, contract, preferred_element_type=f32).astype(bf16),
-            "dp",
-            scatter_dimension=0,
-            tiled=True,
+            jnp.concatenate(grads, axis=1), "dp", scatter_dimension=0, tiled=True
         )
 
-    def spread(grad):
-        return lax.all_to_all(grad, "seq", 0, 1, tiled=True).astype(f32)
-
-    g_down = weight_grad(cot_low, active_low)
-    grad_active = jnp.dot(cot_low, w_down, preferred_element_type=f32)
+    grad_active = jnp.dot(cot_low, ffn[:, ffn_width:], preferred_element_type=f32)
     grad_inner_low = active_pull(grad_active)[0].astype(bf16)
-    grad_second = row_scatter(contract_last(grad_inner_low, w_in))
-    g_in = weight_grad(second_low, grad_inner_low)
+    ffn_grads, grad_inner_low, active_low = lax.optimization_barrier(
+        (
+            jnp.concatenate(
+                [product(second_low, grad_inner_low), product(cot_low, active_low)], axis=1
+            ),
+            grad_inner_low,
+            active_low,
+        )
+    )
+    ffn_grads = reduce_dp([ffn_grads])
+    grad_second = exact_scatter(grad_inner_low, ffn, 5)
     grad_hidden_ln, gain_two, bias_two = second_pull(grad_second)
     grad_hidden = cotangent.astype(f32) + grad_hidden_ln
-    grad_branch_low = row_gather(grad_hidden.astype(bf16))
-    g_out = weight_grad(grad_branch_low, gated_low)
+    grad_branch_low = row_gather(grad_hidden.astype(bf16), 6)
     grad_gated = jnp.dot(grad_branch_low, w_out, preferred_element_type=f32)
     grad_gate, grad_grouped = gating_pull(grad_gated)
     grad_gate_low = grad_gate.astype(bf16)
-    g_g = weight_grad(first_low, grad_gate_low)
+    side_grads, ffn_grads = lax.optimization_barrier(
+        (
+            jnp.concatenate(
+                [product(first_low, grad_gate_low), product(grad_branch_low, gated_low)], axis=1
+            ),
+            ffn_grads,
+        )
+    )
+    side_grads = reduce_dp([side_grads])
     grad_mixed_low = blocked(group_pull(grad_grouped.reshape(length, heads, VD))[0].astype(bf16))
     grad_attn = jnp.einsum(
         "bthv,bshv->bhts", grad_mixed_low, value_low, preferred_element_type=f32
@@ -405,33 +799,27 @@
     )
     grad_value = grad_value + jnp.einsum("bthd,bhdv->bthv", key_scaled, grad_own, precision=highest)
     grad_v_low = grad_value.reshape(length, heads * VD).astype(bf16)
-    g_v = weight_grad(first_low, grad_v_low)
     grad_query_raw = rotate_pull(grad_query.reshape(length, heads * QK))[0]
     grad_key_raw = rotate_pull(grad_key.reshape(length, heads * QK))[0]
-    grad_qk_low = jnp.concatenate([grad_query_raw.astype(bf16), grad_key_raw.astype(bf16)], axis=1)
-    grad_first = row_scatter(
-        contract_last(grad_qk_low, w_qk)
-        + contract_last(grad_v_low, w_v)
-        + contract_last(grad_gate_low, w_g)
-    )
-    g_qk = weight_grad(first_low, grad_qk_low)
+    grad_project_low = jnp.concatenate(
+        [grad_query_raw.astype(bf16), grad_key_raw.astype(bf16), grad_v_low, grad_gate_low], axis=1
+    )
+    qkv_grads, grad_project_low, active_low = lax.optimization_barrier(
+        (product(first_low, grad_project_low[:, :v_end]), grad_project_low, active_low)
+    )
+    qkv_grads = reduce_dp([qkv_grads])
+    grad_first = row_scatter(grad_project_low, mix, 7)
     grad_input_ln, gain_one, bias_one = first_pull(grad_first)
     grad_tokens = grad_hidden + grad_input_ln
-    grad_weights = jnp.concatenate(
-        [
-            spread(g_qk[:, : heads * QK]),
-            spread(g_qk[:, heads * QK :]),
-            spread(g_v),
-            spread(g_g),
-            spread(g_in),
-            spread(g_out),
-            spread(g_down),
-        ],
-        axis=1,
-    )
-    grad_gain, grad_bias = lax.psum(
-        (jnp.stack([gain_one, gain_two]), jnp.stack([bias_one, bias_two])), ("dp", "seq")
-    )
+    result = (hidden + row_scatter(active_low, ffn, 8, column=1)).astype(bf16)
+    g_in, g_down = row_exchange(ffn_grads, (ffn_width, ffn_width), 9)
+    g_g, g_out = row_exchange(side_grads, (heads * VD, heads * VD), 10)
+    g_q, g_k, g_v = row_exchange(qkv_grads, (heads * QK, heads * QK, heads * VD), 12)
+    grad_weights = jnp.concatenate([g_q, g_k, g_v, g_g, g_in, g_out, g_down], axis=1).astype(f32)
+    norms = device_total(
+        jnp.stack([gain_one, gain_two, bias_one, bias_two] * 2), lax.axis_size("dp"), 13
+    )
+    grad_gain, grad_bias = norms[:2], norms[2:4]
     return (result, grad_tokens, grad_weights, grad_gain, grad_bias)
 
 
@@ -444,9 +832,10 @@
         P("dp", None),
         P(("dp", "seq"), None),
     )
-    divides = HEADS % mesh.shape["seq"] == 0
+    dp_size = mesh.shape["dp"]
+    fits = mesh.shape["seq"] == HEADS == 8 and dp_size & (dp_size - 1) == 0
     return jax.shard_map(
-        per_device_heads if divides else per_device_spread,
+        per_device_heads if fits else per_device_spread,
         mesh=mesh,
         in_specs=placed,
         out_specs=(

time: 1180 us -> 684 us (0.58)
  waiting for transfers between devices: 760 us -> 27.2 us
  Pallas kernels: 0 us -> 425 us
  matrix products: 211 us -> 114 us
  blocking collectives: 49.5 us -> 0 us
  starting transfers between devices: 23.2 us -> 0.24 us
  local copies, waits for them, and re-layouts: 49.3 us -> 30 us
    pallas_call x0 -> x12, Pallas kernels: none -> 425 us  [the longest x4 199 us: row_scatter(): pl.pallas_call(functools.partial(scatter_kernel, tile, exact), out_shape=...]
    reduce_scatter x10 -> x3, waiting for transfers between devices: 320 us -> 0.04 us  [reduce_dp(): lax.psum_scatter(jnp.concatenate(grads, axis=1), 'dp', scatter_dimension=...]
    all_gather x4 -> x0, waiting for transfers between devices: 199 us -> none  [row_gather(): return lax.all_gather(part, 'seq', axis=0, tiled=True)]
    all_gather x6 -> x3, waiting for transfers between devices: 206 us -> 26.4 us  [gather_weights(): return lax.all_gather(part, 'dp', axis=0, tiled=True)]
    dot_general x17 -> x10, matrix products: 173 us -> 83 us  [the longest x5 43.8 us: product(): lax.dot_general(left, right, contract, preferred_element_type=f32)]
    psum x1 -> x0, blocking collectives: 40.1 us -> none  [per_device_heads(): lax.psum((jnp.stack([gain_one, gain_two]), jnp.stack([bias_one, bias_two]...]
    all_to_all x6 -> x0, waiting for transfers between devices: 32.5 us -> none  [spread(): return lax.all_to_all(grad, 'seq', 0, 1, tiled=True).astype(f32)]
    all_to_all x6 -> x0, starting transfers between devices: 21.5 us -> none  [spread(): return lax.all_to_all(grad, 'seq', 0, 1, tiled=True).astype(f32)]
  transfers between devices with their start and end apart: 26 -> 6, of which waited for: 20 -> 2; matrix products, arithmetic and copies ran while one was open for 22% -> 22% of each run, Pallas kernels for 0% -> 60%
where the time goes in v2:
time: 684 us; the launch traced here: 679 us
  Pallas kernels  425 us (62%)
  matrix products  114 us (17%)
  other arithmetic  65.1 us (10%)
  local copies, waits for them, and re-layouts  30 us (4%)
  waiting for transfers between devices  27.2 us (4%)
  between operations  17.6 us (3%)
    pallas_call x4, Pallas kernels, row_scatter(): pl.pallas_call(functools.partial(scatter_kernel, tile, exact), out_shape=...  199 us
    pallas_call x4, Pallas kernels, row_gather(): pl.pallas_call(functools.partial(gather_kernel, chunks), out_shape=jax.Sh...  160 us
    pallas_call x3, Pallas kernels, row_exchange(): pl.pallas_call(functools.partial(exchange_kernel, widths), out_shape=[jax...  45.1 us
    dot_general x5, matrix products, product(): lax.dot_general(left, right, contract, preferred_element_type=f32)  43.8 us
    all_gather x3, waiting for transfers between devices, gather_weights(): return lax.all_gather(part, 'dp', axis=0, tiled=True)  26.4 us
    pallas_call x1, Pallas kernels, device_total(): pl.pallas_call(functools.partial(total_kernel, stages), out_shape=jax.Sha...  21.7 us
    unnamed x117, local copies, waits for them, and re-layouts  19.5 us
    dot_general x1, matrix products, per_device_heads(): project = jnp.dot(first_low, mix, preferred_element_type=f32)  17.5 us
  transfers between devices with their start and end apart: 6, of which 2 were waited for; matrix products, arithmetic and copies ran while one was open for 22% of the time, Pallas kernels for 60%

profile of v2, /device:TPU:0, one launch (start us, length us, event | category | flops | bytes accessed | tf_op | source)
XLA Modules:
  0.0 679.5 jit_solution(11034190563564224184)
XLA Ops:
  8.3 2.7 constant_dynamic-slice_fusion.1
  11.0 1.2 pad_maximum_fusion.3
  13.1 1.1 pad_maximum_fusion.6
  17.8 1.2 multiply_exponential_fusion
  24.5 1.4 fusion.38.own
  25.9 41.5 %row_gather_1.1 = bf16[8,256,2048]{2,1,0:T(8,128)(2,1)} custom-call(bf16[256,2048]{1,0:T(8,128)(2,1)} %fusion.38.own), custom_call_target="tpu_custom_call" | custom-call | bytes 120000000 | tf_op jit(solution)/shard_map/row_gather_1/pallas_call | solution.py:344
  67.6 39.8 %row_gather_2.1 = bf16[8,256,2048]{2,1,0:T(8,128)(2,1)} custom-call(bf16[256,2048]{1,0:T(8,128)(2,1)} %own.1), custom_call_target="tpu_custom_call" | custom-call | bytes 120000000 | tf_op jit(solution)/shard_map/row_gather_2/pallas_call | solution.py:344
  107.3 1.3 fusion.105
  108.6 1.2 fusion.103
  110.7 19.8 %all-gather.4.cloned.1.call-done.right = bf16[2048,1536]{1,0:T(8,128)(2,1)} async-done(((bf16[512,1536]{1,0:T(8,128)(2,1)}), bf16[2048,1536]{1,0:T(8,128)(2,1)}) %all-gather.4.cloned.1.call-update) | async-done | bytes 6291472 | tf_op jit(solution)/shard_map/all_gather | solution.py:651
  130.5 17.5 %fusion.124 = f32[2048,1536]{1,0:T(8,128)S(1)} fusion(bf16[2048,2048]{1,0:T(8,128)(2,1)} %bitcast.217, bf16[2048,1536]{1,0:T(8,128)(2,1)} %all-gather.4.cloned.1.call-done.right), kind=kOutput, calls=%fused_computation.244 | convolution fusion | flops 12884901888 | bytes 27262976 | tf_op jit(solution)/shard_map/dot_general | solution.py:669
  149.0 4.9 fusion.80
  154.2 2.3 fusion.53
  158.0 1.4 bitcast_dynamic-update-slice_fusion.8
  160.1 1.4 bitcast_dynamic-update-slice_fusion.6
  162.2 1.2 multiply_convert_fusion.3
  164.4 1.1 bitcast_reduce_fusion
  166.4 1.2 copy-done.7
  167.6 1.7 multiply_convert_fusion.1.left
  169.7 6.6 all-gather.6.cloned.1.call-done.right
  176.3 52.8 %row_scatter_3.1 = (f32[256,2048]{1,0:T(8,128)S(1)}, f32[16,2048]{1,0:T(8,128)S(1)}) custom-call(bf16[2048,512]{1,0:T(8,128)(2,1)S(1)} %multiply_convert_fusion.1.left, bf16[2048,512]{1,0:T(8,128)(2,1)} %all-gather.6.cloned.1.call-done.right, bf16[16,512]{1,0:T(8,128)(2,1)S(1)} %convolution_convert_fusion.5.refs_0_), custom_call_target="tpu_custom_call" | custom-call | flops 4294967296 | bytes 120000000 | tf_op jit(solution)/shard_map/row_scatter_3/pallas_call | solution.py:510
  231.2 1.4 add_convert_fusion.5.own
  232.6 39.8 %row_gather_4.1 = bf16[8,256,2048]{2,1,0:T(8,128)(2,1)} custom-call(bf16[256,2048]{1,0:T(8,128)(2,1)} %add_convert_fusion.5.own), custom_call_target="tpu_custom_call" | custom-call | bytes 120000000 | tf_op jit(solution)/shard_map/row_gather_4/pallas_call | solution.py:344
  272.4 8.4 %multiply_convert_fusion = (bf16[2048,512]{1,0:T(8,128)(2,1)S(1)}, f32[2048,512]{1,0:T(8,128)S(1)}) fusion(bf16[2048,2048]{1,0:T(8,128)(2,1)} %bitcast.226, bf16[2048,1024]{1,0:T(8,128)(2,1)} %all-gather.8.cloned.1.call-done.right), kind=kOutput, calls=%fused_computation.43 | convolution fusion | flops 4304404480 | bytes 16777216 | tf_op jit(solution)/shard_map/dot_general | solution.py:723
  280.8 11.1 %fusion.34 = bf16[2048,512]{1,0:T(8,128)(2,1)S(1)} fusion(bf16[2048,512]{1,0:T(8,128)(2,1)S(1)} %get-tuple-element.30.left, bf16[2048,2048]{1,0:T(8,128)(2,1)} %bitcast.222), kind=kOutput, calls=%fused_computation.61 | convolution fusion | flops 4296015872 | bytes 12582912 | tf_op jit(solution)/shard_map/dot_general | solution.py:729
  291.9 10.8 %fusion.6.left = bf16[2048,512]{1,0:T(8,128)(2,1)S(1)} fusion(f32[2048,512]{1,0:T(8,128)S(1)} %get-tuple-element.122, bf16[2048,2048]{1,0:T(8,128)(2,1)} %bitcast.223, bf16[2048,1024]{1,0:T(8,128)(2,1)S(1)} %copy-done.48), kind=kOutput, calls=%fused_computation.11 | convolution fusion | flops 4315938816 | bytes 16777216 | tf_op jit(solution)/shard_map/dot_general | solution.py:736
  302.6 1.3 copy-done
  304.0 4.8 convolution_convert_fusion.3
  308.8 2.6 pad_maximum_fusion.1
  311.4 2.2 convolution_convert_fusion.4.refs_0_
  313.6 53.1 %row_scatter_5.1 = (f32[256,2048]{1,0:T(8,128)S(1)}, f32[16,2048]{1,0:T(8,128)S(1)}) custom-call(bf16[2048,512]{1,0:T(8,128)(2,1)S(1)} %copy-done.1, bf16[2048,1024]{1,0:T(8,128)(2,1)} %all-gather.8.cloned.1.call-done.right, bf16[16,512]{1,0:T(8,128)(2,1)S(1)} %convolution_convert_fusion.4.refs_0_), custom_call_target="tpu_custom_call" | custom-call | flops 4294967296 | bytes 120000000 | tf_op jit(solution)/shard_map/row_scatter_5/pallas_call | solution.py:510
  366.7 1.6 multiply_reduce_fusion.1
  368.4 1.4 fusion.115
  369.8 1.3 copy-done.13
  371.1 1.3 fusion.74.own
  372.4 38.6 %row_gather_6.1 = bf16[8,256,2048]{2,1,0:T(8,128)(2,1)} custom-call(bf16[256,2048]{1,0:T(8,128)(2,1)} %fusion.74.own), custom_call_target="tpu_custom_call" | custom-call | bytes 120000000 | tf_op jit(solution)/shard_map/row_gather_6/pallas_call | solution.py:344
  411.0 12.4 %multiply_reduce_fusion = (f32[2048]{0:T(1024)S(1)}, f32[2048,512]{1,0:T(8,128)S(1)}) fusion(f32[8,1,512,256]{2,3,0,1:T(8,128)} %copy-done.7, f32[2048]{0:T(1024)S(1)} %bitcast.241, f32[2048,1536]{1,0:T(8,128)} %copy-done.15, bf16[2048,2048]{1,0:T(8,128)(2,1)} %bitcast.224, bf16[2048,512]{1,0:T(8,128)(2,1)} %all-gather.6.cloned.1.call-done.right), kind=kOutput, calls=%fused_computation.42 | convolution fusion | flops 4303353856 | bytes 23085056 | tf_op jit(solution)/shard_map/dot_general | solution.py:752
  423.4 5.7 fusion.114
  429.5 1.6 copy-done.19
  431.1 2.6 fusion.50
  433.7 4.1 fusion.93
  440.9 1.2 multiply_convert_fusion.2
  443.8 1.1 copy-done.21
  445.8 2.5 fusion.45
  448.3 5.2 fusion.83
  453.7 4.6 fusion.16
  459.2 3.3 pad_maximum_fusion.left
  462.5 1.7 slice-done.1
  464.2 10.8 %fusion.27 = bf16[2048,1024]{1,0:T(8,128)(2,1)} fusion(bf16[2048,2048]{1,0:T(8,128)(2,1)S(1)} %bitcast.221, bf16[2048,512]{1,0:T(8,128)(2,1)S(1)} %bitcast.232, bf16[2048,256]{1,0:T(8,128)(2,1)S(1)} %fusion.88, bf16[2048,256]{1,0:T(8,128)(2,1)S(1)} %fusion.87), kind=kOutput, calls=%fused_computation.47 | convolution fusion | flops 8604614656 | bytes 16777216 | tf_op jit(solution)/shard_map/dot_general | solution.py:729
  475.1 8.7 %convolution_convert_fusion = bf16[2048,512]{1,0:T(8,128)(2,1)S(1)} fusion(bf16[2048,2048]{1,0:T(8,128)(2,1)} %bitcast.225, bf16[2048,512]{1,0:T(8,128)(2,1)S(1)} %multiply_convert_fusion.1.left), kind=kOutput, calls=%fused_computation.57 | convolution fusion | flops 4296015872 | bytes 12582912 | tf_op jit(solution)/shard_map/dot_general | solution.py:729
  483.8 8.5 %convolution_convert_fusion.1 = bf16[2048,512]{1,0:T(8,128)(2,1)S(1)} fusion(bf16[2048,2048]{1,0:T(8,128)(2,1)} %bitcast.218, bf16[2048,512]{1,0:T(8,128)(2,1)S(1)} %copy-done.25), kind=kOutput, calls=%fused_computation.58 | convolution fusion | flops 4296015872 | bytes 12582912 | tf_op jit(solution)/shard_map/dot_general | solution.py:729
  492.3 2.7 pad_maximum_fusion.2
  495.1 49.2 %row_scatter_7.1 = f32[256,2048]{1,0:T(8,128)S(1)} custom-call(bf16[2048,1536]{1,0:T(8,128)(2,1)} %pad_maximum_fusion.left, bf16[2048,1536]{1,0:T(8,128)(2,1)} %all-gather.4.cloned.1.call-done.right), custom_call_target="tpu_custom_call" | custom-call | flops 12884901888 | bytes 120000000 | tf_op jit(solution)/shard_map/row_scatter_7/pallas_call | solution.py:510
  546.7 21.7 %device_total_13.1 = f32[8,2048]{1,0:T(8,128)} custom-call(f32[8,2048]{1,0:T(8,128)} %stack.79.own), custom_call_target="tpu_custom_call" | custom-call | bytes 30000000 | tf_op jit(solution)/shard_map/device_total_13/pallas_call | solution.py:615
  568.4 1.6 copy-done.3
  570.0 43.7 %row_scatter_8.1 = f32[256,2048]{1,0:T(8,128)S(1)} custom-call(bf16[2048,512]{1,0:T(8,128)(2,1)S(1)} %copy-done.3, bf16[2048,1024]{1,0:T(8,128)(2,1)} %all-gather.8.cloned.1.call-done.right), custom_call_target="tpu_custom_call" | custom-call | flops 4294967296 | bytes 120000000 | tf_op jit(solution)/shard_map/row_scatter_8/pallas_call | solution.py:510
  614.3 1.2 add_convert_fusion.2
  616.5 2.2 add_add_fusion.3
  618.8 14.9 %row_exchange_9.1 = (bf16[64,4096]{1,0:T(8,128)(2,1)}, bf16[64,4096]{1,0:T(8,128)(2,1)}) custom-call(bf16[512,1024]{1,0:T(8,128)(2,1)} %reduce-scatter.6.cloned.1.call-done.grad), custom_call_target="tpu_custom_call" | custom-call | bytes 30000000 | tf_op jit(solution)/shard_map/row_exchange_9/pallas_call | solution.py:577
  633.7 15.4 %row_exchange_12.1 = (bf16[64,2048]{1,0:T(8,128)(2,1)}, bf16[64,2048]{1,0:T(8,128)(2,1)}, bf16[64,4096]{1,0:T(8,128)(2,1)}) custom-call(bf16[512,1024]{1,0:T(8,128)(2,1)} %reduce-scatter.4.cloned.1.call-done.grad), custom_call_target="tpu_custom_call" | custom-call | bytes 30000000 | tf_op jit(solution)/shard_map/row_exchange_12/pallas_call | solution.py:577
  651.1 1.1 constant_dynamic-update-slice_fusion.4
  652.2 14.7 %row_exchange_10.1 = (bf16[64,4096]{1,0:T(8,128)(2,1)}, bf16[64,4096]{1,0:T(8,128)(2,1)}) custom-call(bf16[512,1024]{1,0:T(8,128)(2,1)} %reduce-scatter.8.cloned.1.call-done.grad), custom_call_target="tpu_custom_call" | custom-call | bytes 30000000 | tf_op jit(solution)/shard_map/row_exchange_10/pallas_call | solution.py:577
  666.9 1.2 constant_dynamic-update-slice_fusion.3
  669.3 3.1 convert_element_type.270
  (193 shorter events, 32.2 us)
Async XLA Ops:
  7.2 123.3 %all-gather.4.cloned.1.call-start = ((), (), s32[]{:S(2)}) async-start(), calls=%async_computation.3 | async-start | bytes 7864320 | tf_op jit(solution)/shard_map/all_gather | solution.py:651
  12.3 2.6 copy-start.37
  12.3 164.0 %all-gather.6.cloned.1.call-start = ((), (), s32[]{:S(2)}) async-start(), calls=%async_computation.4 | async-start | bytes 2621440 | tf_op jit(solution)/shard_map/all_gather | solution.py:651
  12.3 8.1 %copy-start.9 = (bf16[256,2048]{1,0:T(8,128)(2,1)S(1)}, bf16[256,2048]{1,0:T(8,128)(2,1)}, u32[]{:S(2)}) copy-start(bf16[256,2048]{1,0:T(8,128)(2,1)} %param.6) | copy-start | bytes 3145732
  13.0 259.3 %all-gather.8.cloned.1.call-start = ((), (), s32[]{:S(2)}) async-start(), calls=%async_computation.5 | async-start | bytes 5242880 | tf_op jit(solution)/shard_map/all_gather | solution.py:651
  14.2 9.5 %copy-start.40 = (f32[2,2048]{1,0:T(2,128)S(1)}, f32[2,2048]{1,0:T(2,128)}, u32[]{:S(2)}) copy-start(f32[2,2048]{1,0:T(2,128)} %param.8) | copy-start | bytes 49156
  14.2 480.8 %reduce-scatter.6.cloned.1.call-start = ((), (), s32[]{:S(2)}) async-start(), calls=%async_computation.7 | async-start | bytes 5242880 | tf_op jit(solution)/shard_map/reduce_scatter | solution.py:732
  17.2 145.0 %copy-start.33 = (pred[256,256]{1,0:T(8,128)(4,1)}, pred[256,256]{1,0:T(8,128)(4,1)S(1)}, u32[]{:S(2)}) copy-start(pred[256,256]{1,0:T(8,128)(4,1)S(1)} %iota_compare_fusion) | copy-start | bytes 196612
  20.6 46.9 %copy-start.35 = (f32[256]{0:T(256)}, f32[256]{0:T(256)S(1)}, u32[]{:S(2)}) copy-start(f32[256]{0:T(256)S(1)} %broadcast_multiply_fusion.2) | copy-start | bytes 3076
  21.1 1.9 copy-start.41
  21.1 46.4 %copy-start.38 = (f32[256]{0:T(256)}, f32[256]{0:T(256)S(1)}, u32[]{:S(2)}) copy-start(f32[256]{0:T(256)S(1)} %fusion.107) | copy-start | bytes 3076
  23.7 43.8 %copy-start.30 = (f32[1,2048]{1,0:T(1,128)}, f32[1,2048]{1,0:T(1,128)S(1)}, u32[]{:S(2)}) copy-start(f32[1,2048]{1,0:T(1,128)S(1)} %get-tuple-element.94) | copy-start | bytes 24580
  67.5 42.3 %copy-start.47 = (s32[7]{0:T(128)S(1)}, s32[7]{0:T(128)}, u32[]{:S(2)}) copy-start(s32[7]{0:T(128)} %get-tuple-element.105) | copy-start | bytes 88
  67.5 42.4 %copy-start.44 = (f32[256]{0:T(256)S(1)}, f32[256]{0:T(256)}, u32[]{:S(2)}) copy-start(f32[256]{0:T(256)} %get-tuple-element.125) | copy-start | bytes 3076
  148.0 18.4 %copy-start.15 = (f32[2048,1536]{1,0:T(8,128)}, f32[2048,1536]{1,0:T(8,128)S(1)}, u32[]{:S(2)}) copy-start(f32[2048,1536]{1,0:T(8,128)S(1)} %fusion.124) | copy-start | bytes 37748740
  148.3 15.1 %copy-start.11 = (bf16[2048,512]{1,0:T(8,128)(2,1)}, bf16[2048,512]{1,0:T(8,128)(2,1)S(1)}, u32[]{:S(2)}) copy-start(bf16[2048,512]{1,0:T(8,128)(2,1)S(1)} %slice.355) | copy-start | bytes 6291460
  148.3 0.7 copy-start.45
  154.2 8.1 %copy-start.16 = (bf16[2048,1,256]{2,0,1:T(8,128)(2,1)}, bf16[2048,1,256]{2,0,1:T(8,128)(2,1)S(1)}, u32[]{:S(2)}) copy-start(bf16[2048,1,256]{2,0,1:T(8,128)(2,1)S(1)} %get-tuple-element.132) | copy-start | bytes 3145732
  154.2 10.2 %copy-start.18 = (bf16[2048,1,256]{2,0,1:T(8,128)(2,1)}, bf16[2048,1,256]{2,0,1:T(8,128)(2,1)S(1)}, u32[]{:S(2)}) copy-start(bf16[2048,1,256]{2,0,1:T(8,128)(2,1)S(1)} %get-tuple-element.131) | copy-start | bytes 3145732
  162.2 2.2 copy-start.20
  163.4 1.0 copy-start.26
  165.5 2.0 copy-start.7
  167.6 1.7 copy-start.43
  229.8 1.3 copy-start.4
  280.7 11.1 %copy-start.2 = (bf16[2048,512]{1,0:T(8,128)(2,1)}, bf16[2048,512]{1,0:T(8,128)(2,1)S(1)}, u32[]{:S(2)}) copy-start(bf16[2048,512]{1,0:T(8,128)(2,1)S(1)} %get-tuple-element.30.left) | copy-start | bytes 6291460
  280.8 11.1 %copy-start.48 = (bf16[2048,1024]{1,0:T(8,128)(2,1)S(1)}, bf16[2048,1024]{1,0:T(8,128)(2,1)}, u32[]{:S(2)}) copy-start(bf16[2048,1024]{1,0:T(8,128)(2,1)} %all-gather.8.cloned.1.call-done.right) | copy-start | bytes 12582916
  280.8 23.2 %slice-start.2 = ((s8[8388608]{0:T(1024)(128)(4,1)}), s8[4194304]{0:T(1024)(128)(4,1)S(1)}, s32[]{:S(2)}) async-start(s8[8388608]{0:T(1024)(128)(4,1)} %bitcast.227), calls=%async_computation.11 | async-start | bytes 8388608
  291.9 12.1 %slice-start.3 = ((s8[8388608]{0:T(1024)(128)(4,1)}), s8[4194304]{0:T(1024)(128)(4,1)S(1)}, s32[]{:S(2)}) async-start(s8[8388608]{0:T(1024)(128)(4,1)} %bitcast.227), calls=%async_computation.12 | async-start | bytes 8388608
  302.6 1.3 copy-start
  311.4 322.3 %reduce-scatter.4.cloned.1.call-start = ((), (), s32[]{:S(2)}) async-start(), calls=%async_computation.6 | async-start | bytes 5242880 | tf_op jit(solution)/shard_map/reduce_scatter | solution.py:732
  311.4 2.2 copy-start.1
  313.6 53.1 %copy-start.5 = (f32[256,2048]{1,0:T(8,128)S(1)}, f32[256,2048]{1,0:T(8,128)}, u32[]{:S(2)}) copy-start(f32[256,2048]{1,0:T(8,128)} %copy-done.4) | copy-start | bytes 6291460
  368.4 2.7 copy-start.22
  369.8 1.3 copy-start.13
  411.0 12.4 %copy-start.8 = (f32[8,1,512,256]{2,3,0,1:T(8,128)S(1)}, f32[8,1,512,256]{2,3,0,1:T(8,128)}, u32[]{:S(2)}) copy-start(f32[8,1,512,256]{2,3,0,1:T(8,128)} %copy-done.7) | copy-start | bytes 12582916
  429.1 30.0 %copy-start.24 = (bf16[2048,512]{1,0:T(8,128)(2,1)}, bf16[2048,512]{1,0:T(8,128)(2,1)S(1)}, u32[]{:S(2)}) copy-start(bf16[2048,512]{1,0:T(8,128)(2,1)S(1)} %get-tuple-element.72) | copy-start | bytes 6291460
  429.2 2.0 copy-start.19
  439.3 1.6 copy-start.12
  439.3 1.6 copy-start.34
  442.1 1.2 copy-start.17
  443.3 1.6 copy-start.21
  445.7 2.5 copy-start.46
  453.7 4.6 copy-start.27
  458.4 4.2 slice-start
  459.2 5.1 slice-start.1
  475.0 177.1 %reduce-scatter.8.cloned.1.call-start = ((), (), s32[]{:S(2)}) async-start(), calls=%async_computation.8 | async-start | bytes 5242880 | tf_op jit(solution)/shard_map/reduce_scatter | solution.py:732
  475.1 8.8 %copy-start.25 = (bf16[2048,512]{1,0:T(8,128)(2,1)S(1)}, bf16[2048,512]{1,0:T(8,128)(2,1)}, u32[]{:S(2)}) copy-start(bf16[2048,512]{1,0:T(8,128)(2,1)} %copy-done.24) | copy-start | bytes 6291460
  495.1 49.3 %copy-start.10 = (bf16[256,2048]{1,0:T(8,128)(2,1)S(1)}, bf16[256,2048]{1,0:T(8,128)(2,1)}, u32[]{:S(2)}) copy-start(bf16[256,2048]{1,0:T(8,128)(2,1)} %param.6) | copy-start | bytes 3145732
  495.1 49.2 %copy-start.31 = (f32[1,2048]{1,0:T(1,128)S(1)}, f32[1,2048]{1,0:T(1,128)}, u32[]{:S(2)}) copy-start(f32[1,2048]{1,0:T(1,128)} %copy-done.30) | copy-start | bytes 24580
  495.1 49.2 %copy-start.36 = (f32[256]{0:T(256)S(1)}, f32[256]{0:T(256)}, u32[]{:S(2)}) copy-start(f32[256]{0:T(256)} %copy-done.35) | copy-start | bytes 3076
  544.3 0.7 copy-start.42
  544.3 0.7 copy-start.39
  568.4 1.6 copy-start.3
  570.0 43.7 %copy-start.32 = (f32[8,2048]{1,0:T(8,128)S(1)}, f32[8,2048]{1,0:T(8,128)}, u32[]{:S(2)}) copy-start(f32[8,2048]{1,0:T(8,128)} %device_total_13.1) | copy-start | bytes 196612
  570.0 44.3 %copy-start.6 = (f32[256,2048]{1,0:T(8,128)S(1)}, f32[256,2048]{1,0:T(8,128)}, u32[]{:S(2)}) copy-start(f32[256,2048]{1,0:T(8,128)} %copy-done.4) | copy-start | bytes 6291460
  614.3 2.0 copy-start.14
  614.3 2.2 copy-start.23
  666.9 2.3 copy-start.29
  666.9 2.3 copy-start.28
Sparse Core Ops, SparseCore 0:
  12.4 118.0 all-gather.3
  132.1 44.1 all-gather.5
  177.8 79.5 all-gather.7
  311.5 74.7 reduce-scatter.5
  475.1 74.7 reduce-scatter.3
  552.1 77.9 reduce-scatter.7
